TPU v7x, 256 devices: a whole 4x4x8 slice. The times are simulated.
256 devices in a mesh: wide: 64 (over z, x, core), narrow: 4 (over y).
Axes of the slice: x: 4, y: 4, z: 8, core: 2. Of those that a mesh axis runs over, the one named last changes fastest.
Arguments:
- teacher_attn: bfloat16 [512, 2048], P(None, 'narrow'), may hold values from -60 to 60
- out_proj: bfloat16 [2048, 4608], P('narrow', 'wide'), may hold values from -0.125 to 0.125
- teacher_resid: bfloat16 [512, 4608], P(None, 'wide'), may hold values from -60 to 60
- norm_gains: float32 [2, 4608], replicated, may hold values from 0.5 to 1.5
- teacher_embed: bfloat16 [129024, 4608], P(('wide', 'narrow')), may hold values from -0.375 to 0.375
- student_hidden: bfloat16 [512, 3584], P('wide'), may hold values from -6 to 6
- student_embed: bfloat16 [129024, 3584], P(('wide', 'narrow')), may hold values from -0.375 to 0.375
- token_ids: int32 [512], replicated, may hold values from 0 to 129023
Outputs:
- loss: float32 [], replicated
- hidden_grad: float32 [512, 3584], P(('wide', 'narrow'))
- embed_grad: bfloat16 [129024, 3584], P(('wide', 'narrow'))
All inputs are finite; a program needn't handle non-finite values.
Results may differ from a plain program's by a relative error of at most 0.0075.
Values may be sent and summed in bfloat16 or wider, within the bound.
A program may use at most 128 MiB of HBM per device.

v0:
```python
import jax
import jax.numpy as jnp
from jax import lax
from jax.sharding import PartitionSpec as P

DT = 4608


def capped(left, right):
    product = lax.dot_general(
        left, right, (((1,), (1,)), ((), ())), preferred_element_type=jnp.float32
    )
    return 30.0 * jnp.tanh(product / 30.0)


def body(
    teacher_attn,
    out_proj,
    teacher_resid,
    norm_gains,
    teacher_embed,
    student_hidden,
    student_embed,
    token_ids,
):
    partial_out = jnp.dot(teacher_attn, out_proj, preferred_element_type=jnp.float32)
    attn_out = lax.psum(partial_out, "narrow").astype(jnp.bfloat16)
    width_here = teacher_resid.shape[1]
    feature_start = lax.axis_index("wide") * width_here
    gains_here = lax.dynamic_slice_in_dim(norm_gains, feature_start, width_here, 1)
    attn_wide = lax.optimization_barrier(attn_out).astype(jnp.float32)
    post_sum = lax.psum(jnp.sum(attn_wide * attn_wide, axis=1), "wide")
    post_scale = lax.rsqrt(post_sum / DT + 1e-06)
    mixed = teacher_resid.astype(jnp.float32) + gains_here[0] * (attn_wide * post_scale[:, None])
    final_sum = lax.psum(jnp.sum(mixed * mixed, axis=1), "wide")
    final_scale = lax.rsqrt(final_sum / DT + 1e-06)
    local_final = (gains_here[1] * (mixed * final_scale[:, None])).astype(jnp.bfloat16)
    teacher_final = lax.all_gather(local_final, "wide", axis=1, tiled=True)
    student_full = lax.all_gather(student_hidden, "wide", axis=0, tiled=True)
    teach = capped(teacher_final, teacher_embed)
    stud = capped(student_full, student_embed)
    exp_teach = jnp.exp(teach - 30.0)
    exp_stud = jnp.exp(stud - 30.0)
    vocab_rows = teacher_embed.shape[0]
    offset = lax.axis_index(("wide", "narrow")) * vocab_rows
    columns = lax.broadcasted_iota(jnp.int32, stud.shape, 1)
    onehot = (columns == (token_ids - offset)[:, None]).astype(jnp.float32)
    zt, zs, cross, target = lax.psum(
        (
            jnp.sum(exp_teach, axis=1),
            jnp.sum(exp_stud, axis=1),
            jnp.sum(exp_teach * (teach - stud), axis=1),
            jnp.sum(onehot * stud, axis=1),
        ),
        ("wide", "narrow"),
    )
    per_token = cross / zt - jnp.log(zt) + jnp.log(zs) + jnp.log(zs) + 30.0 - target
    loss = jnp.mean(per_token)
    tokens_all = stud.shape[0]
    grad_logit = 2.0 * exp_stud / zs[:, None] - exp_teach / zt[:, None] - onehot
    grad_z = (grad_logit * (1.0 - (stud / 30.0) ** 2) / tokens_all).astype(jnp.bfloat16)
    hidden_grad = lax.psum_scatter(
        jnp.dot(grad_z, student_embed, preferred_element_type=jnp.float32),
        ("wide", "narrow"),
        scatter_dimension=0,
        tiled=True,
    )
    embed_grad = lax.dot_general(
        grad_z, student_full, (((0,), (0,)), ((), ())), preferred_element_type=jnp.float32
    ).astype(jnp.bfloat16)
    return (loss, hidden_grad, embed_grad)


def solution(mesh):
    in_specs = (
        P(None, "narrow"),
        P("narrow", "wide"),
        P(None, "wide"),
        P(),
        P(("wide", "narrow"), None),
        P("wide", None),
        P(("wide", "narrow"), None),
        P(),
    )
    out_specs = (P(), P(("wide", "narrow"), None), P(("wide", "narrow"), None))
    return jax.shard_map(body, mesh=mesh, in_specs=in_specs, out_specs=out_specs, check_vma=False)
```

profile of v0, /device:TPU:1, one launch (start us, length us, event | category | flops | bytes accessed | tf_op | source)
XLA Modules:
  0.0 729.1 jit_solution(14730126540036818566)
XLA Ops:
  7.2 0.0 all-gather.5.cloned.1.call-start
  7.2 0.7 all-gather.5.cloned.1.call-update
  7.9 0.0 all-gather.3.cloned.1.call-start
  8.0 0.2 copy-done
  8.2 1.2 fusion.12
  9.4 15.8 %all-reduce.6 = bf16[512,72]{0,1:T(8,128)(2,1)S(1)} all-reduce(f32[512,72]{0,1:T(8,128)S(1)} %fusion.12), channel_id=1, replica_groups=mesh['wide'=64,'narrow'=4] {'narrow'}, use_global_device_ids=true, to_apply=%region_0.0 | all-reduce | flops 36864 | bytes 221184 | tf_op jit(solution)/shard_map/psum | solution.py:27
  25.2 131.1 %psum.50 = f32[512]{0:T(512)S(1)} all-reduce(f32[512]{0:T(512)S(1)} %fusion.5), channel_id=1, replica_groups=mesh['wide'=64,'narrow'=4] {'wide'}, use_global_device_ids=true, to_apply=%region_2.0 | all-reduce | flops 512 | bytes 4096 | tf_op jit(solution)/shard_map/psum | solution.py:32
  156.3 0.8 constant_dynamic-slice_fusion.1
  157.0 1.0 multiply_reduce_fusion.1
  158.0 125.0 %psum.51 = f32[512]{0:T(512)S(1)} all-reduce(f32[512]{0:T(512)S(1)} %multiply_reduce_fusion.1), channel_id=1, replica_groups=mesh['wide'=64,'narrow'=4] {'wide'}, use_global_device_ids=true, to_apply=%region_4.0 | all-reduce | flops 512 | bytes 4096 | tf_op jit(solution)/shard_map/psum | solution.py:35
  283.0 1.6 multiply_convert_fusion.1
  284.6 0.0 all-gather.3.cloned.1.call-update
  284.6 0.0 all-reduce.5.cloned.1.call-start
  284.7 0.7 broadcast_subtract_fusion
  285.4 5.2 fusion
  290.6 68.8 %all-gather.3.cloned.1.call-done = bf16[512,4608]{0,1:T(8,128)(2,1)} async-done(((bf16[512,72]{0,1:T(8,128)(2,1)}), bf16[512,4608]{0,1:T(8,128)(2,1)}) %all-gather.3.cloned.1.call-update) | async-done | bytes 4718608 | tf_op jit(solution)/shard_map/all_gather | solution.py:38
  359.4 6.8 multiply_reduce_fusion
  366.2 75.4 %all-reduce.1 = (f32[512]{0:T(512)S(1)}, f32[512]{0:T(512)S(1)}, f32[512]{0:T(512)S(1)}, f32[512]{0:T(512)S(1)}) all-reduce(f32[512]{0:T(512)S(1)} %get-tuple-element.5, f32[512]{0:T(512)S(1)} %get-tuple-element.4, f32[512]{0:T(512)S(1)} %get-tuple-element.6, ...), channel_id=1, replica_groups=mesh['wide'=64,'narrow'=4] {'wide','narrow'}, use_global_device_ids=true, to_apply=%region_12.0 | all-reduce | flops 2048 | bytes 16384 | tf_op jit(solution)/shard_map/psum | solution.py:48
  441.6 7.6 %fusion.11 = f32[512,3584]{1,0:T(8,128)} fusion(bf16[504,3584]{1,0:T(8,128)(2,1)} %param.14, f32[512,504]{0,1:T(8,128)S(1)} %fusion, f32[512,504]{0,1:T(8,128)S(1)} %get-tuple-element.13, f32[512]{0:T(512)S(1)} %get-tuple-element.9, f32[512]{0:T(512)S(1)} %get-tuple-element.8, s32[512]{0:T(512)S(1)} %broadcast_subtract_fusion), kind=kOutput, calls=%fused_computation.32 | convolution fusion | flops 1853558784 | bytes 13023232 | tf_op jit(solution)/shard_map/dot_general | solution.py:63
  449.2 0.0 all-reduce.5.cloned.1.call-update
  449.3 0.6 fusion.10
  450.5 6.3 convolution_convert_fusion
  456.8 263.1 %all-reduce.5.cloned.1.call-done = f32[512,3584]{1,0:T(8,128)} async-done(((f32[512,3584]{1,0:T(8,128)}), f32[512,3584]{1,0:T(8,128)}) %all-reduce.5.cloned.1.call-update) | async-done | bytes 7340048
  719.9 1.5 constant_dynamic-slice_fusion
  (6 shorter events, 0.1 us)
Async XLA Ops:
  7.2 1.0 copy-start
  7.2 278.2 %all-gather.5.cloned.1.call-start = ((), (), s32[]{:S(2)}) async-start(), calls=%async_computation.1 | async-start | bytes 3727360 | tf_op jit(solution)/shard_map/all_gather | solution.py:39
  7.9 351.5 %all-gather.3.cloned.1.call-start = ((), (), s32[]{:S(2)}) async-start(), calls=%async_computation | async-start | bytes 4792320 | tf_op jit(solution)/shard_map/all_gather | solution.py:38
  284.6 435.3 %all-reduce.5.cloned.1.call-start = ((), (), s32[]{:S(2)}) async-start(), calls=%async_computation.2 | async-start | bytes 14680064
Sparse Core Ops, SparseCore 0:
  10.8 82.8 all-gather.4
  284.8 74.5 all-gather.2
  449.4 270.4 all-reduce.4
where the time goes:
time: 730 us; the launch traced here: 729 us
  blocking collectives  347 us (48%)
  waiting for transfers between devices  333 us (46%)
  matrix products  27.1 us (4%)
  between operations  15.6 us (2%)
    unnamed x4, waiting for transfers between devices  264 us
    psum x1, blocking collectives, body(): post_sum = lax.psum(jnp.sum(attn_wide * attn_wide, axis=1), 'wide')  131 us
    psum x1, blocking collectives, body(): final_sum = lax.psum(jnp.sum(mixed * mixed, axis=1), 'wide')  125 us
    psum x1, blocking collectives, body(): lax.psum((jnp.sum(exp_teach, axis=1), jnp.sum(exp_stud, axis=1), jnp.sum(...  75.4 us
    all_gather x1, waiting for transfers between devices, body(): teacher_final = lax.all_gather(local_final, 'wide', axis=1, tiled=True)  68.8 us
    psum x1, blocking collectives, body(): attn_out = lax.psum(partial_out, 'narrow').astype(jnp.bfloat16)  15.8 us
  transfers between devices with their start and end apart: 3, of which 2 were waited for; matrix products, arithmetic and copies ran while one was open for 2% of the time, Pallas kernels for 0%

commit v1 on v0

v1 whole, which is shorter than its diff:
```python
import jax
import jax.numpy as jnp
from jax import lax
from jax.experimental import pallas as pl
from jax.experimental.pallas import tpu as pltpu
from jax.sharding import PartitionSpec as P

TOK, DT, DS, V, F = 512, 4608, 3584, 504, 72
NZ, NX, NY = 8, 4, 4
SA = 2048
TA = 80
HA = 2560
HB = DS - HA
NSEM = 192
MESH = pl.DeviceIdType.MESH
f32, bf16 = jnp.float32, jnp.bfloat16


def dot(a, b, ca, cb):
    return lax.dot_general(a, b, (((ca,), (cb,)), ((), ())), preferred_element_type=f32)


def kernel(
    attn_h, oproj_h, resid_h, gains_h, te_h, sh_h, se_h, ids_h,
    loss_o, hg_o, eg_o,
    attn, oproj, resid, gains, te, sh, se, ids,
    sf, tf, shx, shr, pt, pr, scale, sums, sums2, sr1, sr2, fx, fr,
    sb, tb, esb, etb, st, st2, st3, q1, q2, q3, dz,
    ho, hs, hr, hc, x1r, z1r, y1, y1b, z2r, x2r, fs0, fs1, fr0, fr1, eg,
    lsem, ss, rs,
):
    w = lax.axis_index("wide")
    y = lax.axis_index("narrow")
    z, x, c = w // 8, (w // 2) % 4, w % 2

    def dev(z_, x_, c_, y_):
        return ((z_ * 4 + x_) * 2 + c_, y_)

    def zp(k):
        return dev((z + k + NZ) % NZ, x, c, y)

    def xp(k):
        return dev(z, (x + k + NX) % NX, c, y)

    def yp(k):
        return dev(z, x, c, (y + k) % NY)

    def xcp(k):
        q = (x * 2 + c + k) % 8
        return dev(z, q // 2, q % 2, y)

    sib = dev(z, x, 1 - c, y)

    counter = [0]

    def sem():
        counter[0] += 1
        return counter[0] - 1

    class Copy:
        def __init__(self, src, dst, to, landing=None):
            self.src, self.dst, self.to, self.i = src, dst, to, sem()
            self.landing = dst if landing is None else landing

        def make(self, dst):
            return pltpu.make_async_remote_copy(
                src_ref=self.src, dst_ref=dst, send_sem=ss.at[self.i], recv_sem=rs.at[self.i],
                device_id=self.to, device_id_type=MESH,
            )

        def start(self):
            self.make(self.dst).start()

        def wait_send(self):
            self.make(self.dst).wait_send()

        def wait_recv(self):
            self.make(self.landing).wait_recv()

    def on_core(which, fn):
        pl.when(c == which)(fn)

    local = [
        pltpu.make_async_copy(a, b, lsem.at[i])
        for i, (a, b) in enumerate(
            [(sh_h, sh), (attn_h, attn), (oproj_h, oproj), (resid_h, resid), (gains_h, gains), (ids_h, ids), (se_h, se), (te_h, te)]
        )
    ]
    for cp in local:
        cp.start()

    barrier = pltpu.get_barrier_semaphore()
    peers = [zp(k) for k in range(1, 8)] + [xcp(k) for k in range(1, 8)] + [yp(k) for k in range(1, 4)]
    peers += [dev(z, x, 1 - c, (y + k) % NY) for k in range(1, 4)]
    for p in peers:
        pl.semaphore_signal(barrier, inc=1, device_id=p, device_id_type=MESH)
    local[0].wait()
    shx[...] = sh[...].astype(f32)
    pl.semaphore_wait(barrier, len(peers))

    c_sh = Copy(shx, shr, sib)
    c_sh.start()

    def ring(n, pos, peer, block, half):
        m = n // 2
        waits, starts, every = {}, {}, []
        for s in range(1, m + 1):
            last = s == m
            pick = half if last else (lambda i, h: block(i))
            r = Copy(pick((pos - s + 1 + n) % n, 0), pick((pos - s + 1 + n) % n, 0), peer(1), pick((pos - s + n) % n, 0))
            l = Copy(pick((pos + s - 1) % n, 1), pick((pos + s - 1) % n, 1), peer(-1), pick((pos + s) % n, 1))
            starts[s] = [r.start, l.start]
            waits[s] = [r.wait_recv, l.wait_recv]
            every += [r.wait_send, l.wait_send]
        return starts, waits, every

    def gather(buf, sel):
        def at(i, j, core, h=None):
            rows, cols = sel(core, h)
            return buf.at[i, j, rows, cols]

        every = slice(None)
        z0 = ring(NZ, z, zp, lambda i: at(i, x, 0), lambda i, h: at(i, x, 0, h))
        x0 = ring(NX, x, xp, lambda i: at(every, i, 0), lambda i, h: at(every, i, 0, h))
        x1 = ring(NX, x, xp, lambda i: at(z, i, 1), lambda i, h: at(z, i, 1, h))
        z1 = ring(NZ, z, zp, lambda i: at(i, every, 1), lambda i, h: at(i, every, 1, h))
        s0 = {k: Copy(at(every, (x + k + NX) % NX, 0), at(every, (x + k + NX) % NX, 0), sib) for k in (0, 1, -1, 2)}
        s1 = {
            k: Copy(at((z + k + NZ) % NZ, every, 1), at((z + k + NZ) % NZ, every, 1), sib)
            for k in (0, 1, -1, 2, -2, 3, -3, 4)
        }
        steps0 = [
            z0[0][1],
            z0[1][1] + z0[0][2],
            z0[1][2] + z0[0][3],
            z0[1][3] + z0[0][4],
            z0[1][4] + x0[0][1] + [s0[0].start],
            x0[1][1] + x0[0][2] + [s0[1].start, s0[-1].start],
            x0[1][2] + [s0[2].start],
            [s1[k].wait_recv for k in s1],
        ]
        steps1 = [
            x1[0][1],
            x1[1][1] + x1[0][2],
            x1[1][2] + z1[0][1] + [s1[0].start],
            z1[1][1] + z1[0][2] + [s1[1].start, s1[-1].start],
            z1[1][2] + z1[0][3] + [s1[2].start, s1[-2].start],
            z1[1][3] + z1[0][4] + [s1[3].start, s1[-3].start],
            z1[1][4] + [s1[4].start],
            [s0[k].wait_recv for k in s0],
        ]
        drain0 = z0[2] + x0[2] + [s0[k].wait_send for k in s0]
        drain1 = x1[2] + z1[2] + [s1[k].wait_send for k in s1]

        def emit(fns0, fns1):
            def run0():
                for fn in fns0:
                    fn()

            def run1():
                for fn in fns1:
                    fn()

            on_core(0, run0)
            on_core(1, run1)

        def gen():
            for a, b in zip(steps0, steps1):
                emit(a, b)
                yield

        return gen(), lambda: emit(drain0, drain1)

    def student_sel(core, h):
        lo, hi = (0, SA) if core == 0 else (SA, DS)
        if h is not None:
            mid = (lo + hi) // 2
            lo, hi = (lo, mid) if h == 0 else (mid, hi)
        return slice(None), pl.ds(lo, hi - lo)

    def teacher_sel(core, h):
        rows = pl.ds(0, TA) if core == 0 else pl.ds(TA, 2 * F - TA)
        return rows, slice(None) if h is None else pl.ds(h * 256, 256)

    student, student_drain = gather(sf, student_sel)
    teacher, teacher_drain = gather(tf, teacher_sel)

    local[1].wait()
    local[2].wait()
    proj = dot(oproj[...], attn[...], 0, 1)
    for b in range(NY):
        pt[b] = proj[:, b * 128 : (b + 1) * 128]
    c_pr = [Copy(pt.at[(y + k) % NY], pr.at[k - 1], yp(k)) for k in range(1, NY)]
    for cp in c_pr:
        cp.start()

    c_sh.wait_recv()
    first = jnp.where(c == 0, shx[...], shr[...])
    second = jnp.where(c == 0, shr[...], shx[...])
    block = jnp.concatenate([first, second], axis=0).astype(bf16)

    def put0():
        sf[z, x, :, 0:SA] = block[:, 0:SA]

    def put1():
        sf[z, x, :, SA:DS] = block[:, SA:DS]

    on_core(0, put0)
    on_core(1, put1)
    next(student)

    local[4].wait()
    feature = w * F + lax.broadcasted_iota(jnp.int32, (F, 512), 0)
    lane = lax.broadcasted_iota(jnp.int32, (F, 512), 1)

    def pick_gains(i, carry):
        part = gains[:, pl.ds(pl.multiple_of(i * 512, 512), 512)]
        here = (lane + i * 512) == feature
        g0 = carry[0] + jnp.sum(jnp.where(here, part[0:1, :], 0.0), axis=1, keepdims=True)
        g1 = carry[1] + jnp.sum(jnp.where(here, part[1:2, :], 0.0), axis=1, keepdims=True)
        return g0, g1

    zero_col = jnp.zeros((F, 1), f32)
    g0, g1 = lax.fori_loop(0, DT // 512, pick_gains, (zero_col, zero_col))
    local[3].wait()
    rows_here = resid[pl.ds(pl.multiple_of(y * 128, 128), 128), :]
    eye = (
        lax.broadcasted_iota(jnp.int32, (128, 128), 0) == lax.broadcasted_iota(jnp.int32, (128, 128), 1)
    ).astype(bf16)
    r = dot(rows_here, eye, 0, 0)

    for cp in c_pr:
        cp.wait_recv()
    a = pt[y] + pr[0] + pr[1] + pr[2]
    a = a.astype(bf16).astype(f32)
    ga = g0 * a
    sums[...] = jnp.zeros_like(sums)
    sums[0:1, :] = jnp.sum(a * a, axis=0, keepdims=True)
    sums[1:2, :] = jnp.sum(r * r, axis=0, keepdims=True)
    sums[2:3, :] = jnp.sum(r * ga, axis=0, keepdims=True)
    sums[3:4, :] = jnp.sum(ga * ga, axis=0, keepdims=True)
    c_s1 = [Copy(sums, sr1.at[k - 1], zp(k)) for k in range(1, 8)]
    for cp in c_s1:
        cp.start()
    next(student)
    for cp in c_s1:
        cp.wait_recv()
    sums2[...] = sums[...] + jnp.sum(sr1[...], axis=0)
    c_s2 = [Copy(sums2, sr2.at[k - 1], xcp(k)) for k in range(1, 8)]
    for cp in c_s2:
        cp.start()
    next(student)
    for cp in c_s2:
        cp.wait_recv()
    total = sums2[...] + jnp.sum(sr2[...], axis=0)
    post = lax.rsqrt(total[0:1, :] / DT + 1e-06)
    square = total[1:2, :] + 2.0 * post * total[2:3, :] + post * post * total[3:4, :]
    fin = lax.rsqrt(jnp.maximum(square, 0.0) / DT + 1e-06)
    final = g1 * ((r + ga * post) * fin)
    fx[...] = final
    c_f = Copy(fx, fr, sib)
    c_f.start()
    c_f.wait_recv()
    lo = jnp.where(c == 0, final, fr[...])
    hi = jnp.where(c == 0, fr[...], final)
    both = jnp.concatenate([lo, hi], axis=0).astype(bf16)
    mine = pl.ds(pl.multiple_of(y * 128, 128), 128)
    c_y0 = []
    c_y1 = []
    for k in range(1, NY):
        theirs = pl.ds(pl.multiple_of((y - k + NY) % NY * 128, 128), 128)
        for core, out in ((0, c_y0), (1, c_y1)):
            rows = teacher_sel(core, None)[0]
            out.append(Copy(tf.at[z, x, rows, mine], tf.at[z, x, rows, mine], yp(k), tf.at[z, x, rows, theirs]))

    def spread0():
        tf[z, x, 0:TA, mine] = both[0:TA]
        for cp in c_y0:
            cp.start()

    def spread1():
        tf[z, x, TA : 2 * F, mine] = both[TA : 2 * F]
        for cp in c_y1:
            cp.start()

    on_core(0, spread0)
    on_core(1, spread1)
    next(student)

    def spread_wait0():
        for cp in c_y0:
            cp.wait_recv()

    def spread_wait1():
        for cp in c_y1:
            cp.wait_recv()

    on_core(0, spread_wait0)
    on_core(1, spread_wait1)
    next(teacher)
    for _ in range(4):
        next(student)

    local[6].wait()
    for k in range(7):
        cols = slice(k * 512, (k + 1) * 512)
        part = dot(se[:, cols], sf[:, :, :, cols].reshape(TOK, 512), 1, 1)
        sb[...] = part if k == 0 else sb[...] + part
        next(teacher)

    local[7].wait()
    for k in range(4):
        part = dot(te[:, k * 1152 : (k + 1) * 1152], tf[2 * k : 2 * k + 2].reshape(1152, TOK), 1, 0)
        tb[...] = part if k == 0 else tb[...] + part

    local[5].wait()
    token = ids[...] - (w * NY + y) * V
    row = lax.broadcasted_iota(jnp.int32, (56, TOK), 0)

    def fold(v):
        return jnp.sum(v.reshape(7, 8, TOK), axis=0)

    def stats(i, carry):
        rows = pl.ds(pl.multiple_of(i * 56, 8), 56)
        s = 30.0 * jnp.tanh(sb[rows, :] / 30.0)
        t = 30.0 * jnp.tanh(tb[rows, :] / 30.0)
        es = jnp.exp(s - 30.0)
        et = jnp.exp(t - 30.0)
        sb[rows, :] = s
        esb[rows, :] = es
        etb[rows, :] = et
        hit = jnp.where(row + i * 56 == token, s, 0.0)
        return (
            carry[0] + fold(et),
            carry[1] + fold(es),
            carry[2] + fold(et * (t - s)),
            carry[3] + fold(hit),
        )

    zero = jnp.zeros((8, TOK), f32)
    accs = lax.fori_loop(0, V // 56, stats, (zero, zero, zero, zero))
    st[...] = jnp.zeros_like(st)
    for i in range(4):
        st[i : i + 1, :] = jnp.sum(accs[i], axis=0, keepdims=True)

    c_q1 = [Copy(st, q1.at[k - 1], zp(k)) for k in range(1, 8)]
    c_q2 = [Copy(st2, q2.at[k - 1], xcp(k)) for k in range(1, 8)]
    c_q3 = [Copy(st3, q3.at[k - 1], yp(k)) for k in range(1, 4)]
    for cp in c_q1:
        cp.start()
    for cp in c_q1:
        cp.wait_recv()
    st2[...] = st[...] + jnp.sum(q1[...], axis=0)
    for cp in c_q2:
        cp.start()
    for cp in c_q2:
        cp.wait_recv()
    st3[...] = st2[...] + jnp.sum(q2[...], axis=0)
    for cp in c_q3:
        cp.start()
    for cp in c_q3:
        cp.wait_recv()
    all_stats = st3[...] + jnp.sum(q3[...], axis=0)
    zt, zs = all_stats[0:1, :], all_stats[1:2, :]
    cross, target = all_stats[2:3, :], all_stats[3:4, :]
    log_zs = jnp.log(zs)
    per_token = cross / zt - jnp.log(zt) + log_zs + log_zs + 30.0 - target
    loss_o[...] = jnp.broadcast_to(jnp.sum(per_token, axis=1, keepdims=True) / TOK, loss_o.shape)

    scale[0:1, :] = 1.0 / zt
    scale[1:2, :] = 2.0 / zs
    for k in range(4):
        cols = slice(k * 128, (k + 1) * 128)
        s = sb[:, cols]
        row_all = lax.broadcasted_iota(jnp.int32, (V, 128), 0)
        onehot = (row_all == token[:, cols]).astype(f32)
        u = s / 30.0
        g = scale[1:2, cols] * esb[:, cols] - scale[0:1, cols] * etb[:, cols] - onehot
        dz[:, cols] = (g * (1.0 - u * u) / TOK).astype(bf16)

    def product(lo, n, out):
        def step(j, _):
            cols = pl.ds(pl.multiple_of(lo + j * 256, 256), 256)
            val = dot(dz[...], se[:, cols], 0, 0)
            out(pl.ds(pl.multiple_of(j * 256, 256), 256), val.reshape(NZ, NX, 16, 256))
            return 0

        lax.fori_loop(0, n // 256, step, 0)

    def out_send(cols, val):
        hs[:, :, :, cols] = val.astype(bf16)

    def out_own(cols, val):
        ho[:, :, :, cols] = val

    every = slice(None)
    chunks0 = [pl.ds(j * 512, 512) for j in range(HA // 512)]
    c_d0 = [Copy(hs.at[every, every, every, pl.ds(0, HB)], hr.at[every, every, every, pl.ds(0, HB)], sib)]
    c_d1 = [Copy(hs.at[every, every, every, ch], hr.at[every, every, every, ch], sib) for ch in chunks0]
    c_x1 = [
        [Copy(hc.at[every, (x + k) % NX, every, ch], x1r.at[k - 1, every, every, ch], xp(k)) for k in range(1, 4)]
        for ch in chunks0
    ]
    c_z1 = [Copy(hc.at[(z + k) % NZ, every, every, pl.ds(0, HB)], z1r.at[k - 1], zp(k)) for k in range(1, 8)]

    def grad0():
        product(HA, HB, out_send)
        c_d0[0].start()
        product(0, HA, out_own)
        for j, ch in enumerate(chunks0):
            cols = slice(j * 512, (j + 1) * 512)
            c_d1[j].wait_recv()
            val = ho[:, :, :, cols] + hr[:, :, :, cols].astype(f32)
            ho[:, :, :, cols] = val
            hc[:, :, :, cols] = val.astype(bf16)
            for cp in c_x1[j]:
                cp.start()

    def grad1():
        for j, ch in enumerate(chunks0):
            def one(cols, val, j=j):
                hs[:, :, :, pl.ds(pl.multiple_of(cols.start + j * 512, 256), 256)] = val.astype(bf16)

            product(j * 512, 512, one)
            c_d1[j].start()
        product(HA, HB, out_own)
        c_d0[0].wait_recv()
        val = ho[:, :, :, 0:HB] + hr[:, :, :, 0:HB].astype(f32)
        ho[:, :, :, 0:HB] = val
        hc[:, :, :, 0:HB] = val.astype(bf16)
        for cp in c_z1:
            cp.start()

    on_core(0, grad0)
    on_core(1, grad1)

    c_eg = []
    for k in range(7):
        cols = slice(k * 512, (k + 1) * 512)
        eg[:, cols] = dot(dz[...], sf[:, :, :, cols].reshape(TOK, 512), 1, 0).astype(bf16)
        c_eg.append(pltpu.make_async_copy(eg.at[:, pl.ds(k * 512, 512)], eg_o.at[:, pl.ds(k * 512, 512)], lsem.at[8 + k]))
        c_eg[k].start()

    c_z2 = [Copy(y1b.at[(z + k) % NZ], z2r.at[k - 1], zp(k)) for k in range(1, 8)]
    to = [(0, k) for k in range(4)] + [(1, k) for k in range(4)]

    def last(fs, frx, core):
        out = []
        for core_, k in to:
            if core_ == core and k == 0:
                continue
            yy = (y + k) % NY
            out.append(Copy(fs.at[pl.ds(8 * core_ + 2 * yy, 2)], frx.at[k], dev(z, x, core_, yy)))
        return out

    c_f0 = last(fs0, fr0, 0)
    c_f1 = last(fs1, fr1, 1)

    def second0():
        for j in range(len(chunks0)):
            for cp in c_x1[j]:
                cp.wait_recv()
        for j in range(len(chunks0)):
            cols = slice(j * 512, (j + 1) * 512)
            val = ho[:, x, :, cols]
            for k in range(3):
                val = val + x1r[k, :, :, cols].astype(f32)
            y1[:, :, cols] = val
            y1b[:, :, cols] = val.astype(bf16)
        for cp in c_z2:
            cp.start()
        for cp in c_z2:
            cp.wait_recv()
        val = y1[z]
        for k in range(7):
            val = val + z2r[k].astype(f32)
        for t in range(HA // 128):
            fs0[:, t, :] = val[:, t * 128 : (t + 1) * 128]
        for cp in c_f0:
            cp.start()
        fr0[0] = fs0[pl.ds(2 * y, 2)]

    c_x2b = [Copy(y1b.at[(x + k) % NX, every, pl.ds(0, HB)], x2r.at[k - 1], xp(k)) for k in range(1, 4)]

    def second1():
        for cp in c_z1:
            cp.wait_recv()
        val = ho[z, :, :, 0:HB]
        for k in range(7):
            val = val + z1r[k].astype(f32)
        y1[0:NX, :, 0:HB] = val
        y1b[0:NX, :, 0:HB] = val.astype(bf16)
        for cp in c_x2b:
            cp.start()
        for cp in c_x2b:
            cp.wait_recv()
        val = y1[x, :, 0:HB]
        for k in range(3):
            val = val + x2r[k].astype(f32)
        for t in range(HB // 128):
            fs1[:, t, :] = val[:, t * 128 : (t + 1) * 128]
        for cp in c_f1:
            cp.start()
        fr1[0] = fs1[pl.ds(8 + 2 * y, 2)]

    on_core(0, second0)
    on_core(1, second1)

    def arrive(frx, k, i):
        pltpu.make_async_remote_copy(
            src_ref=frx.at[k], dst_ref=frx.at[k], send_sem=ss.at[i], recv_sem=rs.at[i], device_id=sib, device_id_type=MESH
        ).wait_recv()

    def index_of(copies, core, core_, k):
        order = [(a, b) for a, b in to if not (a == core and b == 0)]
        return copies[order.index((core_, k))].i

    def arrive_on(core):
        def fn():
            for k in range(4):
                if not (core == 0 and k == 0):
                    arrive(fr0, k, index_of(c_f0, 0, core, k))
                if not (core == 1 and k == 0):
                    arrive(fr1, k, index_of(c_f1, 1, core, k))

        return fn

    on_core(0, arrive_on(0))
    on_core(1, arrive_on(1))
    hg_o[:, 0 : HA // 128, :] = jnp.sum(fr0[...], axis=0)
    hg_o[:, HA // 128 : DS // 128, :] = jnp.sum(fr1[...], axis=0)

    student_drain()
    teacher_drain()
    for cp in [c_sh, c_f] + c_pr + c_s1 + c_s2 + c_q1 + c_q2 + c_q3:
        cp.wait_send()

    def end0():
        for cp in c_y0 + c_d0 + [b for a_ in c_x1 for b in a_] + c_z2 + c_f0:
            cp.wait_send()

    def end1():
        for cp in c_y1 + c_d1 + c_z1 + c_x2b + c_f1:
            cp.wait_send()

    on_core(0, end0)
    on_core(1, end1)
    for cp in c_eg:
        cp.wait()
    assert counter[0] <= NSEM


def body(teacher_attn, out_proj, teacher_resid, norm_gains, teacher_embed, student_hidden, student_embed, token_ids):
    hbm = pl.BlockSpec(memory_space=pl.ANY)
    vm = pl.BlockSpec(memory_space=pltpu.VMEM)
    v = pltpu.VMEM
    loss, hg, eg = pl.pallas_call(
        kernel,
        out_shape=(
            jax.ShapeDtypeStruct((8, 128), f32),
            jax.ShapeDtypeStruct((2, DS // 128, 128), f32),
            jax.ShapeDtypeStruct((V, DS), bf16),
        ),
        in_specs=[hbm] * 8,
        out_specs=(vm, vm, hbm),
        scratch_shapes=[
            v((TOK, 512), bf16), v((512, F), bf16), v((TOK, F), bf16), v((2, DT), f32),
            v((V, DT), bf16), v((8, DS), bf16), v((V, DS), bf16), v((1, TOK), jnp.int32),
            v((NZ, NX, 16, DS), bf16), v((NZ, NX, 2 * F, TOK), bf16),
            v((8, DS), f32), v((8, DS), f32),
            v((NY, F, 128), f32), v((NY - 1, F, 128), f32), v((8, TOK), f32),
            v((8, 128), f32), v((8, 128), f32), v((7, 8, 128), f32), v((7, 8, 128), f32),
            v((F, 128), f32), v((F, 128), f32),
            v((V, TOK), f32), v((V, TOK), f32), v((V, TOK), f32), v((V, TOK), f32),
            v((8, TOK), f32), v((8, TOK), f32), v((8, TOK), f32),
            v((7, 8, TOK), f32), v((7, 8, TOK), f32), v((3, 8, TOK), f32),
            v((V, TOK), bf16),
            v((NZ, NX, 16, HA), f32), v((NZ, NX, 16, HA), bf16), v((NZ, NX, 16, HA), bf16), v((NZ, NX, 16, HA), bf16),
            v((3, NZ, 16, HA), bf16), v((7, NX, 16, HB), bf16),
            v((NZ, 16, HA), f32), v((NZ, 16, HA), bf16), v((7, 16, HA), bf16), v((4, 16, HB), bf16),
            v((16, HA // 128, 128), f32), v((16, HB // 128, 128), f32),
            v((4, 2, HA // 128, 128), f32), v((4, 2, HB // 128, 128), f32),
            v((V, DS), bf16),
            pltpu.SemaphoreType.DMA((15,)),
            pltpu.SemaphoreType.DMA((NSEM,)),
            pltpu.SemaphoreType.DMA((NSEM,)),
        ],
        compiler_params=pltpu.CompilerParams(
            collective_id=0, has_side_effects=True, vmem_limit_bytes=60 * 2**20
        ),
        name="step",
    )(
        teacher_attn, out_proj, teacher_resid, norm_gains, teacher_embed, student_hidden, student_embed,
        token_ids.reshape(1, TOK),
    )
    return loss[0, 0], hg.reshape(2, DS), eg


def solution(mesh):
    in_specs = (
        P(None, "narrow"),
        P("narrow", "wide"),
        P(None, "wide"),
        P(),
        P(("wide", "narrow"), None),
        P("wide", None),
        P(("wide", "narrow"), None),
        P(),
    )
    out_specs = (P(), P(("wide", "narrow"), None), P(("wide", "narrow"), None))
    return jax.shard_map(body, mesh=mesh, in_specs=in_specs, out_specs=out_specs, check_vma=False)
```

time: 730 us -> 144 us (0.20)
  blocking collectives: 347 us -> 0 us
  waiting for transfers between devices: 333 us -> 0 us
  Pallas kernels: 0 us -> 134 us
  matrix products: 27.1 us -> 0 us
  between operations: 15.6 us -> 0.64 us
  local copies, waits for them, and re-layouts: 2.53 us -> 9.93 us
    psum x4 -> x0, blocking collectives: 347 us -> none  [the longest x1 131 us: body(): post_sum = lax.psum(jnp.sum(attn_wide * attn_wide, axis=1), 'wide')]
    unnamed x4 -> x0, waiting for transfers between devices: 264 us -> none
    pallas_call x0 -> x1, Pallas kernels: none -> 134 us  [body(): pl.pallas_call(kernel, out_shape=(jax.ShapeDtypeStruct((8, 128), f32), ja...]
    all_gather x2 -> x0, waiting for transfers between devices: 68.8 us -> none  [the longest x1 68.8 us: body(): teacher_final = lax.all_gather(local_final, 'wide', axis=1, tiled=True)]
    dot_general x5 -> x0, matrix products: 27.1 us -> none  [the longest x2 12 us: capped(): lax.dot_general(left, right, (((1,), (1,)), ((), ())), preferred_element_...]
  transfers between devices with their start and end apart: 3 -> 0, of which waited for: 2 -> 0; matrix products, arithmetic and copies ran while one was open for 2% -> 0% of each run, Pallas kernels for 0% -> 0%
where the time goes in v1:
time: 144 us
  Pallas kernels  134 us (93%)
  local copies, waits for them, and re-layouts  9.93 us (7%)
    pallas_call x1, Pallas kernels, body(): pl.pallas_call(kernel, out_shape=(jax.ShapeDtypeStruct((8, 128), f32), ja...  134 us
    unnamed x4, local copies, waits for them, and re-layouts  8.73 us

profile of v1, /device:TPU:1, one launch (start us, length us, event | category | flops | bytes accessed | tf_op | source)
XLA Modules:
  0.0 144.1 jit_solution(13590280427911135071)
XLA Ops:
  0.6 1.6 %copy.13.oproj_h = bf16[512,72]{1,0:T(8,128)(2,1)} copy(bf16[512,72]{0,1:T(8,128)(2,1)} %param.9) | data formatting | bytes 147456 | tf_op args[1]
  2.3 1.6 %copy.14.resid_h = bf16[512,72]{1,0:T(8,128)(2,1)} copy(bf16[512,72]{0,1:T(8,128)(2,1)} %param.10) | data formatting | bytes 147456 | tf_op args[2]
  3.9 133.6 %step.1 = (f32[8,128]{1,0:T(8,128)}, f32[2,28,128]{2,1,0:T(8,128)}, bf16[504,3584]{1,0:T(8,128)(2,1)}) custom-call(bf16[512,512]{1,0:T(8,128)(2,1)} %attn_h.1, bf16[512,72]{1,0:T(8,128)(2,1)} %copy.13.oproj_h, bf16[512,72]{1,0:T(8,128)(2,1)} %copy.14.resid_h, f32[2,4608]{1,0:T(2,128)} %gains_h.1, bf16[504,4608]{1,0:T(8,128)(2,1)} %te_h.1, ...), custom_call_target="tpu_custom_call" | custom-call | tf_op jit(solution)/shard_map/step/pallas_call | solution.py:557
  137.5 1.2 slice.3
  138.7 1.4 copy.17
  140.1 4.1 %copy.19 = bf16[504,3584]{1,0:T(8,128)(2,1)} copy(bf16[504,3584]{1,0:T(8,128)(2,1)} %get-tuple-element.14) | data formatting | bytes 7225344

commit v2 on v1

--- a/solution.py
+++ b/solution.py
@@ -7,11 +7,11 @@
 
 TOK, DT, DS, V, F = 512, 4608, 3584, 504, 72
 NZ, NX, NY = 8, 4, 4
-SA = 2048
-TA = 80
+SA = 1792
+TA = 64
 HA = 2560
 HB = DS - HA
-NSEM = 192
+NSEM = 320
 MESH = pl.DeviceIdType.MESH
 f32, bf16 = jnp.float32, jnp.bfloat16
 
@@ -24,9 +24,9 @@
     attn_h, oproj_h, resid_h, gains_h, te_h, sh_h, se_h, ids_h,
     loss_o, hg_o, eg_o,
     attn, oproj, resid, gains, te, sh, se, ids,
-    sf, tf, shx, shr, pt, pr, scale, sums, sums2, sr1, sr2, fx, fr,
-    sb, tb, esb, etb, st, st2, st3, q1, q2, q3, dz,
-    ho, hs, hr, hc, x1r, z1r, y1, y1b, z2r, x2r, fs0, fs1, fr0, fr1, eg,
+    sf, tf, shx, shr, pt, pr, scale, sums, sums2, sums3, sr1, sr2, fx, fr,
+    sb, tb, esb, etb, st, st2, st3, q1, q2, q3, dz, dzt,
+    ho, hs, hr, hc, x1r, za, zb, ta, tb2, y1, y1b, z2r, x2r, fs0, fs1, fr0, fr1, eg,
     lsem, ss, rs,
 ):
     w = lax.axis_index("wide")
@@ -45,9 +45,8 @@
     def yp(k):
         return dev(z, x, c, (y + k) % NY)
 
-    def xcp(k):
-        q = (x * 2 + c + k) % 8
-        return dev(z, q // 2, q % 2, y)
+    def xyp(k):
+        return dev(z, (x + k // 4) % NX, c, (y + k) % NY)
 
     sib = dev(z, x, 1 - c, y)
 
@@ -90,7 +89,7 @@
         cp.start()
 
     barrier = pltpu.get_barrier_semaphore()
-    peers = [zp(k) for k in range(1, 8)] + [xcp(k) for k in range(1, 8)] + [yp(k) for k in range(1, 4)]
+    peers = [zp(k) for k in range(1, 8)] + [xyp(k) for k in range(1, 16)] + [sib]
     peers += [dev(z, x, 1 - c, (y + k) % NY) for k in range(1, 4)]
     for p in peers:
         pl.semaphore_signal(barrier, inc=1, device_id=p, device_id_type=MESH)
@@ -114,43 +113,70 @@
             every += [r.wait_send, l.wait_send]
         return starts, waits, every
 
+    near = (1, -1, 2, -2, 3, -3, 4)
+
     def gather(buf, sel):
         def at(i, j, core, h=None):
             rows, cols = sel(core, h)
             return buf.at[i, j, rows, cols]
 
         every = slice(None)
+
+        def zi(k):
+            return (z + k + NZ) % NZ
+
+        def xi(k):
+            return (x + k + NX) % NX
+
         z0 = ring(NZ, z, zp, lambda i: at(i, x, 0), lambda i, h: at(i, x, 0, h))
-        x0 = ring(NX, x, xp, lambda i: at(every, i, 0), lambda i, h: at(every, i, 0, h))
-        x1 = ring(NX, x, xp, lambda i: at(z, i, 1), lambda i, h: at(z, i, 1, h))
-        z1 = ring(NZ, z, zp, lambda i: at(i, every, 1), lambda i, h: at(i, every, 1, h))
-        s0 = {k: Copy(at(every, (x + k + NX) % NX, 0), at(every, (x + k + NX) % NX, 0), sib) for k in (0, 1, -1, 2)}
-        s1 = {
-            k: Copy(at((z + k + NZ) % NZ, every, 1), at((z + k + NZ) % NZ, every, 1), sib)
-            for k in (0, 1, -1, 2, -2, 3, -3, 4)
+        x0 = {
+            (d, k): Copy(at(zi(d), x, 0), at(zi(d), x, 0), xp(k), at(zi(d), xi(-k), 0))
+            for d in (0,) + near for k in (1, 2, 3)
         }
+        s0 = {k: Copy(at(every, xi(-k), 0), at(every, xi(-k), 0), sib) for k in (0, 1, 3, 2)}
+
+        def fan(*ds):
+            return [x0[d, k].start for d in ds for k in (1, 3, 2)]
+
+        def landed(k):
+            return [x0[d, k].wait_recv for d in (0,) + near]
+
         steps0 = [
-            z0[0][1],
-            z0[1][1] + z0[0][2],
-            z0[1][2] + z0[0][3],
-            z0[1][3] + z0[0][4],
-            z0[1][4] + x0[0][1] + [s0[0].start],
-            x0[1][1] + x0[0][2] + [s0[1].start, s0[-1].start],
-            x0[1][2] + [s0[2].start],
-            [s1[k].wait_recv for k in s1],
+            z0[0][1] + fan(0),
+            z0[1][1] + z0[0][2] + fan(1, -1),
+            z0[1][2] + z0[0][3] + fan(2, -2),
+            z0[1][3] + z0[0][4] + fan(3, -3),
+            z0[1][4] + fan(4) + [s0[0].start],
+            landed(1) + [s0[1].start] + landed(3) + [s0[3].start],
+            landed(2) + [s0[2].start],
         ]
+        x1 = {k: Copy(at(z, x, 1), at(z, x, 1), xp(k), at(z, xi(-k), 1)) for k in (1, 3, 2)}
+        z1 = {
+            k: ring(NZ, z, zp, lambda i, k=k: at(i, xi(-k), 1), lambda i, h, k=k: at(i, xi(-k), 1, h)) for k in (0, 1, 3, 2)
+        }
+        s1 = {k: Copy(at(zi(k), every, 1), at(zi(k), every, 1), sib) for k in (0,) + near}
+
+        def onward(n):
+            out = []
+            for k in (0, 1, 3, 2):
+                out += z1[k][1][n]
+                if n < 4:
+                    out += z1[k][0][n + 1]
+            return out
+
         steps1 = [
-            x1[0][1],
-            x1[1][1] + x1[0][2],
-            x1[1][2] + z1[0][1] + [s1[0].start],
-            z1[1][1] + z1[0][2] + [s1[1].start, s1[-1].start],
-            z1[1][2] + z1[0][3] + [s1[2].start, s1[-2].start],
-            z1[1][3] + z1[0][4] + [s1[3].start, s1[-3].start],
-            z1[1][4] + [s1[4].start],
-            [s0[k].wait_recv for k in s0],
+            [x1[k].start for k in x1] + z1[0][0][1],
+            sum([[x1[k].wait_recv] + z1[k][0][1] for k in x1], []) + [s1[0].start],
+            onward(1) + [s1[1].start, s1[-1].start],
+            onward(2) + [s1[2].start, s1[-2].start],
+            onward(3) + [s1[3].start, s1[-3].start],
+            onward(4) + [s1[4].start],
+            [],
         ]
-        drain0 = z0[2] + x0[2] + [s0[k].wait_send for k in s0]
-        drain1 = x1[2] + z1[2] + [s1[k].wait_send for k in s1]
+        steps0.append([s1[k].wait_recv for k in s1])
+        steps1.append([s0[k].wait_recv for k in s0])
+        drain0 = z0[2] + [x0[i].wait_send for i in x0] + [s0[k].wait_send for k in s0]
+        drain1 = [x1[k].wait_send for k in x1] + sum([z1[k][2] for k in z1], []) + [s1[k].wait_send for k in s1]
 
         def emit(fns0, fns1):
             def run0():
@@ -187,7 +213,7 @@
 
     local[1].wait()
     local[2].wait()
-    proj = dot(oproj[...], attn[...], 0, 1)
+    proj = dot(oproj[...], attn[...], 1, 1)
     for b in range(NY):
         pt[b] = proj[:, b * 128 : (b + 1) * 128]
     c_pr = [Copy(pt.at[(y + k) % NY], pr.at[k - 1], yp(k)) for k in range(1, NY)]
@@ -223,11 +249,7 @@
     zero_col = jnp.zeros((F, 1), f32)
     g0, g1 = lax.fori_loop(0, DT // 512, pick_gains, (zero_col, zero_col))
     local[3].wait()
-    rows_here = resid[pl.ds(pl.multiple_of(y * 128, 128), 128), :]
-    eye = (
-        lax.broadcasted_iota(jnp.int32, (128, 128), 0) == lax.broadcasted_iota(jnp.int32, (128, 128), 1)
-    ).astype(bf16)
-    r = dot(rows_here, eye, 0, 0)
+    r = resid[:, pl.ds(pl.multiple_of(y * 128, 128), 128)].astype(f32)
 
     for cp in c_pr:
         cp.wait_recv()
@@ -239,20 +261,24 @@
     sums[1:2, :] = jnp.sum(r * r, axis=0, keepdims=True)
     sums[2:3, :] = jnp.sum(r * ga, axis=0, keepdims=True)
     sums[3:4, :] = jnp.sum(ga * ga, axis=0, keepdims=True)
-    c_s1 = [Copy(sums, sr1.at[k - 1], zp(k)) for k in range(1, 8)]
-    for cp in c_s1:
-        cp.start()
-    next(student)
-    for cp in c_s1:
-        cp.wait_recv()
-    sums2[...] = sums[...] + jnp.sum(sr1[...], axis=0)
-    c_s2 = [Copy(sums2, sr2.at[k - 1], xcp(k)) for k in range(1, 8)]
+    c_s1 = Copy(sums, sr1.at[0], sib)
+    c_s1.start()
+    c_s1.wait_recv()
+    sums2[...] = sums[...] + sr1[0]
+    c_s2 = [Copy(sums2, sr1.at[k], xp(k)) for k in range(1, 4)]
     for cp in c_s2:
         cp.start()
     next(student)
     for cp in c_s2:
         cp.wait_recv()
-    total = sums2[...] + jnp.sum(sr2[...], axis=0)
+    sums3[...] = sums2[...] + sr1[1] + sr1[2] + sr1[3]
+    c_s3 = [Copy(sums3, sr2.at[k - 1], zp(k)) for k in range(1, 8)]
+    for cp in c_s3:
+        cp.start()
+    next(student)
+    for cp in c_s3:
+        cp.wait_recv()
+    total = sums3[...] + jnp.sum(sr2[...], axis=0)
     post = lax.rsqrt(total[0:1, :] / DT + 1e-06)
     square = total[1:2, :] + 2.0 * post * total[2:3, :] + post * post * total[3:4, :]
     fin = lax.rsqrt(jnp.maximum(square, 0.0) / DT + 1e-06)
@@ -298,15 +324,20 @@
     on_core(0, spread_wait0)
     on_core(1, spread_wait1)
     next(teacher)
-    for _ in range(4):
-        next(student)
+    next(student)
+    next(teacher)
+    next(student)
+    next(teacher)
+    next(student)
+    next(student)
 
     local[6].wait()
     for k in range(7):
         cols = slice(k * 512, (k + 1) * 512)
         part = dot(se[:, cols], sf[:, :, :, cols].reshape(TOK, 512), 1, 1)
         sb[...] = part if k == 0 else sb[...] + part
-        next(teacher)
+        if k < 5:
+            next(teacher)
 
     local[7].wait()
     for k in range(4):
@@ -339,33 +370,32 @@
 
     zero = jnp.zeros((8, TOK), f32)
     accs = lax.fori_loop(0, V // 56, stats, (zero, zero, zero, zero))
-    st[...] = jnp.zeros_like(st)
     for i in range(4):
-        st[i : i + 1, :] = jnp.sum(accs[i], axis=0, keepdims=True)
-
-    c_q1 = [Copy(st, q1.at[k - 1], zp(k)) for k in range(1, 8)]
-    c_q2 = [Copy(st2, q2.at[k - 1], xcp(k)) for k in range(1, 8)]
-    c_q3 = [Copy(st3, q3.at[k - 1], yp(k)) for k in range(1, 4)]
-    for cp in c_q1:
-        cp.start()
-    for cp in c_q1:
-        cp.wait_recv()
-    st2[...] = st[...] + jnp.sum(q1[...], axis=0)
+        total_i = jnp.sum(accs[i], axis=0, keepdims=True)
+        st[i : i + 1, :] = total_i[:, 0:256]
+        st[4 + i : 5 + i, :] = total_i[:, 256:512]
+    c_q1 = Copy(st, q1, sib)
+    c_q1.start()
+    c_q1.wait_recv()
+    st2[...] = st[...] + q1[...]
+    c_q2 = [Copy(st2, q2.at[k - 1], xyp(k)) for k in range(1, 16)]
     for cp in c_q2:
         cp.start()
     for cp in c_q2:
         cp.wait_recv()
     st3[...] = st2[...] + jnp.sum(q2[...], axis=0)
+    c_q3 = [Copy(st3, q3.at[k - 1], zp(k)) for k in range(1, 8)]
     for cp in c_q3:
         cp.start()
     for cp in c_q3:
         cp.wait_recv()
-    all_stats = st3[...] + jnp.sum(q3[...], axis=0)
+    packed = st3[...] + jnp.sum(q3[...], axis=0)
+    all_stats = jnp.concatenate([packed[0:4], packed[4:8]], axis=1)
     zt, zs = all_stats[0:1, :], all_stats[1:2, :]
     cross, target = all_stats[2:3, :], all_stats[3:4, :]
     log_zs = jnp.log(zs)
     per_token = cross / zt - jnp.log(zt) + log_zs + log_zs + 30.0 - target
-    loss_o[...] = jnp.broadcast_to(jnp.sum(per_token, axis=1, keepdims=True) / TOK, loss_o.shape)
+    loss_o[0, 0] = jnp.sum(per_token) / TOK
 
     scale[0:1, :] = 1.0 / zt
     scale[1:2, :] = 2.0 / zs
@@ -376,12 +406,14 @@
         onehot = (row_all == token[:, cols]).astype(f32)
         u = s / 30.0
         g = scale[1:2, cols] * esb[:, cols] - scale[0:1, cols] * etb[:, cols] - onehot
-        dz[:, cols] = (g * (1.0 - u * u) / TOK).astype(bf16)
+        g = g * (1.0 - u * u) / TOK
+        dz[:, cols] = g.astype(bf16)
+        dzt[cols, :] = g.T.astype(bf16)
 
     def product(lo, n, out):
         def step(j, _):
             cols = pl.ds(pl.multiple_of(lo + j * 256, 256), 256)
-            val = dot(dz[...], se[:, cols], 0, 0)
+            val = dot(dzt[...], se[:, cols], 1, 0)
             out(pl.ds(pl.multiple_of(j * 256, 256), 256), val.reshape(NZ, NX, 16, 256))
             return 0
 
@@ -401,7 +433,17 @@
         [Copy(hc.at[every, (x + k) % NX, every, ch], x1r.at[k - 1, every, every, ch], xp(k)) for k in range(1, 4)]
         for ch in chunks0
     ]
-    c_z1 = [Copy(hc.at[(z + k) % NZ, every, every, pl.ds(0, HB)], z1r.at[k - 1], zp(k)) for k in range(1, 8)]
+    own_b = pl.ds(0, HB)
+    half_b = (pl.ds(0, HB // 2), pl.ds(HB // 2, HB // 2))
+
+    def zi(k):
+        return (z + k + NZ) % NZ
+
+    c_za = [Copy(hc.at[zi(4), every, every, half_b[0]], za.at[0, every, every, half_b[0]], zp(1))]
+    c_zb = [Copy(hc.at[zi(4), every, every, half_b[1]], zb.at[0, every, every, half_b[1]], zp(-1))]
+    for k in range(1, 4):
+        c_za.append(Copy(ta.at[k - 1], za.at[k], zp(1)))
+        c_zb.append(Copy(tb2.at[k - 1], zb.at[k], zp(-1)))
 
     def grad0():
         product(HA, HB, out_send)
@@ -428,20 +470,21 @@
         val = ho[:, :, :, 0:HB] + hr[:, :, :, 0:HB].astype(f32)
         ho[:, :, :, 0:HB] = val
         hc[:, :, :, 0:HB] = val.astype(bf16)
-        for cp in c_z1:
-            cp.start()
+        c_za[0].start()
+        c_zb[0].start()
 
     on_core(0, grad0)
     on_core(1, grad1)
 
     c_eg = []
-    for k in range(7):
+
+    def embed(k):
         cols = slice(k * 512, (k + 1) * 512)
         eg[:, cols] = dot(dz[...], sf[:, :, :, cols].reshape(TOK, 512), 1, 0).astype(bf16)
         c_eg.append(pltpu.make_async_copy(eg.at[:, pl.ds(k * 512, 512)], eg_o.at[:, pl.ds(k * 512, 512)], lsem.at[8 + k]))
         c_eg[k].start()
 
-    c_z2 = [Copy(y1b.at[(z + k) % NZ], z2r.at[k - 1], zp(k)) for k in range(1, 8)]
+    c_z2 = [[Copy(y1b.at[(z + k) % NZ, every, ch], z2r.at[k - 1, every, ch], zp(k)) for k in range(1, 8)] for ch in chunks0]
     to = [(0, k) for k in range(4)] + [(1, k) for k in range(4)]
 
     def last(fs, frx, core):
@@ -456,42 +499,51 @@
     c_f0 = last(fs0, fr0, 0)
     c_f1 = last(fs1, fr1, 1)
 
-    def second0():
-        for j in range(len(chunks0)):
+    c_x2b = [Copy(y1b.at[(x + k) % NX, every, own_b], x2r.at[k - 1], xp(k)) for k in range(1, 4)]
+
+    def first0(j):
+        def fn():
             for cp in c_x1[j]:
                 cp.wait_recv()
-        for j in range(len(chunks0)):
             cols = slice(j * 512, (j + 1) * 512)
             val = ho[:, x, :, cols]
             for k in range(3):
                 val = val + x1r[k, :, :, cols].astype(f32)
             y1[:, :, cols] = val
             y1b[:, :, cols] = val.astype(bf16)
-        for cp in c_z2:
-            cp.start()
-        for cp in c_z2:
-            cp.wait_recv()
-        val = y1[z]
-        for k in range(7):
-            val = val + z2r[k].astype(f32)
-        for t in range(HA // 128):
-            fs0[:, t, :] = val[:, t * 128 : (t + 1) * 128]
-        for cp in c_f0:
-            cp.start()
-        fr0[0] = fs0[pl.ds(2 * y, 2)]
-
-    c_x2b = [Copy(y1b.at[(x + k) % NX, every, pl.ds(0, HB)], x2r.at[k - 1], xp(k)) for k in range(1, 4)]
-
-    def second1():
-        for cp in c_z1:
-            cp.wait_recv()
-        val = ho[z, :, :, 0:HB]
-        for k in range(7):
-            val = val + z1r[k].astype(f32)
-        y1[0:NX, :, 0:HB] = val
-        y1b[0:NX, :, 0:HB] = val.astype(bf16)
+            for cp in c_z2[j]:
+                cp.start()
+
+        return fn
+
+    def first1(n):
+        def fn():
+            c_za[n - 1].wait_recv()
+            c_zb[n - 1].wait_recv()
+            a_, b_ = half_b
+            if n == 1:
+                ta[0, :, :, a_] = (ho[zi(3), :, :, a_] + za[0, :, :, a_].astype(f32)).astype(bf16)
+                ta[0, :, :, b_] = hc[zi(3), :, :, b_]
+                tb2[0, :, :, a_] = hc[zi(-3), :, :, a_]
+                tb2[0, :, :, b_] = (ho[zi(-3), :, :, b_] + zb[0, :, :, b_].astype(f32)).astype(bf16)
+            else:
+                ta[n - 1] = (ho[zi(4 - n), :, :, own_b] + za[n - 1].astype(f32)).astype(bf16)
+                tb2[n - 1] = (ho[zi(n - 4), :, :, own_b] + zb[n - 1].astype(f32)).astype(bf16)
+            c_za[n].start()
+            c_zb[n].start()
+
+        return fn
+
+    def turn1():
+        c_za[3].wait_recv()
+        c_zb[3].wait_recv()
+        val = ho[z, :, :, own_b] + za[3].astype(f32) + zb[3].astype(f32)
+        y1[0:NX, :, own_b] = val
+        y1b[0:NX, :, own_b] = val.astype(bf16)
         for cp in c_x2b:
             cp.start()
+
+    def last1():
         for cp in c_x2b:
             cp.wait_recv()
         val = y1[x, :, 0:HB]
@@ -503,8 +555,29 @@
             cp.start()
         fr1[0] = fs1[pl.ds(8 + 2 * y, 2)]
 
-    on_core(0, second0)
-    on_core(1, second1)
+    def last0():
+        for j in range(len(chunks0)):
+            for cp in c_z2[j]:
+                cp.wait_recv()
+            cols = slice(j * 512, (j + 1) * 512)
+            val = y1[z, :, cols]
+            for k in range(7):
+                val = val + z2r[k, :, cols].astype(f32)
+            for t in range(4):
+                fs0[:, 4 * j + t, :] = val[:, t * 128 : (t + 1) * 128]
+        for cp in c_f0:
+            cp.start()
+        fr0[0] = fs0[pl.ds(2 * y, 2)]
+
+    for k in range(2):
+        embed(k)
+    for n, (f0, f1) in enumerate(
+        [(first0(0), first1(1)), (first0(1), first1(2)), (first0(2), first1(3)), (first0(3), turn1), (first0(4), last1)]
+    ):
+        on_core(0, f0)
+        on_core(1, f1)
+        embed(2 + n)
+    on_core(0, last0)
 
     def arrive(frx, k, i):
         pltpu.make_async_remote_copy(
@@ -527,20 +600,23 @@
 
     on_core(0, arrive_on(0))
     on_core(1, arrive_on(1))
-    hg_o[:, 0 : HA // 128, :] = jnp.sum(fr0[...], axis=0)
-    hg_o[:, HA // 128 : DS // 128, :] = jnp.sum(fr1[...], axis=0)
+    head = jnp.sum(fr0[...], axis=0)
+    tail = jnp.sum(fr1[...], axis=0)
+    for t in range(DS // 128):
+        piece = head[:, t, :] if t < HA // 128 else tail[:, t - HA // 128, :]
+        hg_o[:, t * 128 : (t + 1) * 128] = piece
 
     student_drain()
     teacher_drain()
-    for cp in [c_sh, c_f] + c_pr + c_s1 + c_s2 + c_q1 + c_q2 + c_q3:
+    for cp in [c_sh, c_f, c_s1, c_q1] + c_pr + c_s2 + c_s3 + c_q2 + c_q3:
         cp.wait_send()
 
     def end0():
-        for cp in c_y0 + c_d0 + [b for a_ in c_x1 for b in a_] + c_z2 + c_f0:
+        for cp in c_y0 + c_d0 + [b for a_ in c_x1 + c_z2 for b in a_] + c_f0:
             cp.wait_send()
 
     def end1():
-        for cp in c_y1 + c_d1 + c_z1 + c_x2b + c_f1:
+        for cp in c_y1 + c_d1 + c_za + c_zb + c_x2b + c_f1:
             cp.wait_send()
 
     on_core(0, end0)
@@ -557,26 +633,27 @@
     loss, hg, eg = pl.pallas_call(
         kernel,
         out_shape=(
-            jax.ShapeDtypeStruct((8, 128), f32),
-            jax.ShapeDtypeStruct((2, DS // 128, 128), f32),
+            jax.ShapeDtypeStruct((1, 1), f32),
+            jax.ShapeDtypeStruct((2, DS), f32),
             jax.ShapeDtypeStruct((V, DS), bf16),
         ),
         in_specs=[hbm] * 8,
-        out_specs=(vm, vm, hbm),
+        out_specs=(pl.BlockSpec(memory_space=pltpu.SMEM), vm, hbm),
         scratch_shapes=[
-            v((TOK, 512), bf16), v((512, F), bf16), v((TOK, F), bf16), v((2, DT), f32),
+            v((TOK, 512), bf16), v((F, 512), bf16), v((F, TOK), bf16), v((2, DT), f32),
             v((V, DT), bf16), v((8, DS), bf16), v((V, DS), bf16), v((1, TOK), jnp.int32),
             v((NZ, NX, 16, DS), bf16), v((NZ, NX, 2 * F, TOK), bf16),
             v((8, DS), f32), v((8, DS), f32),
             v((NY, F, 128), f32), v((NY - 1, F, 128), f32), v((8, TOK), f32),
-            v((8, 128), f32), v((8, 128), f32), v((7, 8, 128), f32), v((7, 8, 128), f32),
+            v((8, 128), f32), v((8, 128), f32), v((8, 128), f32), v((4, 8, 128), f32), v((7, 8, 128), f32),
             v((F, 128), f32), v((F, 128), f32),
             v((V, TOK), f32), v((V, TOK), f32), v((V, TOK), f32), v((V, TOK), f32),
-            v((8, TOK), f32), v((8, TOK), f32), v((8, TOK), f32),
-            v((7, 8, TOK), f32), v((7, 8, TOK), f32), v((3, 8, TOK), f32),
-            v((V, TOK), bf16),
+            v((8, 256), f32), v((8, 256), f32), v((8, 256), f32),
+            v((8, 256), f32), v((15, 8, 256), f32), v((7, 8, 256), f32),
+            v((V, TOK), bf16), v((TOK, V), bf16),
             v((NZ, NX, 16, HA), f32), v((NZ, NX, 16, HA), bf16), v((NZ, NX, 16, HA), bf16), v((NZ, NX, 16, HA), bf16),
-            v((3, NZ, 16, HA), bf16), v((7, NX, 16, HB), bf16),
+            v((3, NZ, 16, HA), bf16),
+            v((4, NX, 16, HB), bf16), v((4, NX, 16, HB), bf16), v((3, NX, 16, HB), bf16), v((3, NX, 16, HB), bf16),
             v((NZ, 16, HA), f32), v((NZ, 16, HA), bf16), v((7, 16, HA), bf16), v((4, 16, HB), bf16),
             v((16, HA // 128, 128), f32), v((16, HB // 128, 128), f32),
             v((4, 2, HA // 128, 128), f32), v((4, 2, HB // 128, 128), f32),
@@ -590,10 +667,10 @@
         ),
         name="step",
     )(
-        teacher_attn, out_proj, teacher_resid, norm_gains, teacher_embed, student_hidden, student_embed,
+        teacher_attn, out_proj.T, teacher_resid.T, norm_gains, teacher_embed, student_hidden, student_embed,
         token_ids.reshape(1, TOK),
     )
-    return loss[0, 0], hg.reshape(2, DS), eg
+    return loss.reshape(()), hg, eg
 
 
 def solution(mesh):

time: 144 us -> 114 us (0.79)
  Pallas kernels: 134 us -> 106 us
  local copies, waits for them, and re-layouts: 9.93 us -> 5.43 us
  between operations: 0.64 us -> 2.33 us
    pallas_call x1, Pallas kernels: 134 us -> 106 us  [body(): pl.pallas_call(kernel, out_shape=(jax.ShapeDtypeStruct((1, 1), f32), jax....]
    unnamed x4 -> x2, local copies, waits for them, and re-layouts: 8.73 us -> 5.43 us
where the time goes in v2:
time: 114 us
  Pallas kernels  106 us (93%)
  local copies, waits for them, and re-layouts  5.43 us (5%)
  between operations  2.33 us (2%)
    pallas_call x1, Pallas kernels, body(): pl.pallas_call(kernel, out_shape=(jax.ShapeDtypeStruct((1, 1), f32), jax....  106 us
    unnamed x2, local copies, waits for them, and re-layouts  5.43 us

profile of v2, /device:TPU:1, one launch (start us, length us, event | category | flops | bytes accessed | tf_op | source)
XLA Modules:
  0.0 113.9 jit_solution(16626617807597967271)
XLA Ops:
  0.6 106.1 %step.1 = (f32[1,1]{1,0:T(1,128)}, f32[2,3584]{1,0:T(2,128)}, bf16[504,3584]{1,0:T(8,128)(2,1)}) custom-call(bf16[512,512]{1,0:T(8,128)(2,1)} %attn_h.1, bf16[72,512]{1,0:T(8,128)(2,1)} %bitcast.4, bf16[72,512]{1,0:T(8,128)(2,1)} %bitcast.5, f32[2,4608]{1,0:T(2,128)} %gains_h.1, bf16[504,4608]{1,0:T(8,128)(2,1)} %te_h.1, bf16[8,3584]{1,0:T(8,128)(2,1)} %sh_h.1, ...), custom_call_target="tpu_custom_call" | custom-call | tf_op jit(solution)/shard_map/step/pallas_call | solution.py:633
  107.3 1.4 %copy.15 = f32[2,3584]{1,0:T(2,128)} copy(f32[2,3584]{1,0:T(2,128)} %get-tuple-element.13) | data formatting | bytes 57344
  108.7 4.1 %copy.16 = bf16[504,3584]{1,0:T(8,128)(2,1)} copy(bf16[504,3584]{1,0:T(8,128)(2,1)} %get-tuple-element.14) | data formatting | bytes 7225344

commit v3 on v2

--- a/solution.py
+++ b/solution.py
@@ -9,7 +9,7 @@
 NZ, NX, NY = 8, 4, 4
 SA = 1792
 TA = 64
-HA = 2560
+HA = 2304
 HB = DS - HA
 NSEM = 320
 MESH = pl.DeviceIdType.MESH
@@ -24,7 +24,7 @@
     attn_h, oproj_h, resid_h, gains_h, te_h, sh_h, se_h, ids_h,
     loss_o, hg_o, eg_o,
     attn, oproj, resid, gains, te, sh, se, ids,
-    sf, tf, shx, shr, pt, pr, scale, sums, sums2, sums3, sr1, sr2, fx, fr,
+    sf, tf, shx, shr, pt, pr, scale, sums2, sums3, sr1, sr2, rx, rr, ax, ar,
     sb, tb, esb, etb, st, st2, st3, q1, q2, q3, dz, dzt,
     ho, hs, hr, hc, x1r, za, zb, ta, tb2, y1, y1b, z2r, x2r, fs0, fs1, fr0, fr1, eg,
     lsem, ss, rs,
@@ -99,6 +99,10 @@
 
     c_sh = Copy(shx, shr, sib)
     c_sh.start()
+    local[3].wait()
+    rx[...] = resid[:, pl.ds(pl.multiple_of(y * 128, 128), 128)].astype(f32)
+    c_r = Copy(rx, rr, sib)
+    c_r.start()
 
     def ring(n, pos, peer, block, half):
         m = n // 2
@@ -236,45 +240,50 @@
     next(student)
 
     local[4].wait()
-    feature = w * F + lax.broadcasted_iota(jnp.int32, (F, 512), 0)
-    lane = lax.broadcasted_iota(jnp.int32, (F, 512), 1)
+    feature = (w // 2) * 2 * F + lax.broadcasted_iota(jnp.int32, (2 * F, 128), 0)
+    lane = lax.broadcasted_iota(jnp.int32, (2 * F, 128), 1)
 
     def pick_gains(i, carry):
-        part = gains[:, pl.ds(pl.multiple_of(i * 512, 512), 512)]
-        here = (lane + i * 512) == feature
-        g0 = carry[0] + jnp.sum(jnp.where(here, part[0:1, :], 0.0), axis=1, keepdims=True)
-        g1 = carry[1] + jnp.sum(jnp.where(here, part[1:2, :], 0.0), axis=1, keepdims=True)
-        return g0, g1
-
-    zero_col = jnp.zeros((F, 1), f32)
-    g0, g1 = lax.fori_loop(0, DT // 512, pick_gains, (zero_col, zero_col))
-    local[3].wait()
-    r = resid[:, pl.ds(pl.multiple_of(y * 128, 128), 128)].astype(f32)
+        part = gains[:, pl.ds(pl.multiple_of(i * 128, 128), 128)]
+        here = (lane + i * 128) == feature
+        return carry[0] + jnp.where(here, part[0:1, :], 0.0), carry[1] + jnp.where(here, part[1:2, :], 0.0)
+
+    none = jnp.zeros((2 * F, 128), f32)
+    g0, g1 = lax.fori_loop(0, DT // 128, pick_gains, (none, none))
+    g0 = jnp.sum(g0, axis=1, keepdims=True)
+    g1 = jnp.sum(g1, axis=1, keepdims=True)
+    next(student)
+
+    def both_cores(own, other):
+        return jnp.concatenate([jnp.where(c == 0, own, other), jnp.where(c == 0, other, own)], axis=0)
 
     for cp in c_pr:
         cp.wait_recv()
     a = pt[y] + pr[0] + pr[1] + pr[2]
-    a = a.astype(bf16).astype(f32)
+    ax[...] = a.astype(bf16).astype(f32)
+    c_a = Copy(ax, ar, sib)
+    c_a.start()
+    c_r.wait_recv()
+    r = both_cores(rx[...], rr[...])
+    c_a.wait_recv()
+    a = both_cores(ax[...], ar[...])
     ga = g0 * a
-    sums[...] = jnp.zeros_like(sums)
-    sums[0:1, :] = jnp.sum(a * a, axis=0, keepdims=True)
-    sums[1:2, :] = jnp.sum(r * r, axis=0, keepdims=True)
-    sums[2:3, :] = jnp.sum(r * ga, axis=0, keepdims=True)
-    sums[3:4, :] = jnp.sum(ga * ga, axis=0, keepdims=True)
-    c_s1 = Copy(sums, sr1.at[0], sib)
-    c_s1.start()
-    c_s1.wait_recv()
-    sums2[...] = sums[...] + sr1[0]
-    c_s2 = [Copy(sums2, sr1.at[k], xp(k)) for k in range(1, 4)]
+    sums2[...] = jnp.zeros_like(sums2)
+    sums2[0:1, :] = jnp.sum(a * a, axis=0, keepdims=True)
+    sums2[1:2, :] = jnp.sum(r * r, axis=0, keepdims=True)
+    sums2[2:3, :] = jnp.sum(r * ga, axis=0, keepdims=True)
+    sums2[3:4, :] = jnp.sum(ga * ga, axis=0, keepdims=True)
+    c_s2 = [Copy(sums2, sr1.at[k - 1], xp(k)) for k in range(1, 4)]
     for cp in c_s2:
         cp.start()
     next(student)
     for cp in c_s2:
         cp.wait_recv()
-    sums3[...] = sums2[...] + sr1[1] + sr1[2] + sr1[3]
+    sums3[...] = sums2[...] + sr1[0] + sr1[1] + sr1[2]
     c_s3 = [Copy(sums3, sr2.at[k - 1], zp(k)) for k in range(1, 8)]
     for cp in c_s3:
         cp.start()
+    next(student)
     next(student)
     for cp in c_s3:
         cp.wait_recv()
@@ -283,13 +292,7 @@
     square = total[1:2, :] + 2.0 * post * total[2:3, :] + post * post * total[3:4, :]
     fin = lax.rsqrt(jnp.maximum(square, 0.0) / DT + 1e-06)
     final = g1 * ((r + ga * post) * fin)
-    fx[...] = final
-    c_f = Copy(fx, fr, sib)
-    c_f.start()
-    c_f.wait_recv()
-    lo = jnp.where(c == 0, final, fr[...])
-    hi = jnp.where(c == 0, fr[...], final)
-    both = jnp.concatenate([lo, hi], axis=0).astype(bf16)
+    both = final.astype(bf16)
     mine = pl.ds(pl.multiple_of(y * 128, 128), 128)
     c_y0 = []
     c_y1 = []
@@ -327,16 +330,13 @@
     next(student)
     next(teacher)
     next(student)
-    next(teacher)
-    next(student)
-    next(student)
 
     local[6].wait()
     for k in range(7):
         cols = slice(k * 512, (k + 1) * 512)
         part = dot(se[:, cols], sf[:, :, :, cols].reshape(TOK, 512), 1, 1)
         sb[...] = part if k == 0 else sb[...] + part
-        if k < 5:
+        if k < 6:
             next(teacher)
 
     local[7].wait()
@@ -346,21 +346,22 @@
 
     local[5].wait()
     token = ids[...] - (w * NY + y) * V
-    row = lax.broadcasted_iota(jnp.int32, (56, TOK), 0)
+    row = lax.broadcasted_iota(jnp.int32, (24, TOK), 0)
 
     def fold(v):
-        return jnp.sum(v.reshape(7, 8, TOK), axis=0)
+        return jnp.sum(v.reshape(3, 8, TOK), axis=0)
 
     def stats(i, carry):
-        rows = pl.ds(pl.multiple_of(i * 56, 8), 56)
-        s = 30.0 * jnp.tanh(sb[rows, :] / 30.0)
-        t = 30.0 * jnp.tanh(tb[rows, :] / 30.0)
+        rows = pl.ds(pl.multiple_of(i * 24, 8), 24)
+        u = jnp.tanh(sb[rows, :] * (1.0 / 30.0))
+        s = 30.0 * u
+        t = 30.0 * jnp.tanh(tb[rows, :] * (1.0 / 30.0))
         es = jnp.exp(s - 30.0)
         et = jnp.exp(t - 30.0)
-        sb[rows, :] = s
+        sb[rows, :] = 1.0 - u * u
         esb[rows, :] = es
         etb[rows, :] = et
-        hit = jnp.where(row + i * 56 == token, s, 0.0)
+        hit = jnp.where(row + i * 24 == token, s, 0.0)
         return (
             carry[0] + fold(et),
             carry[1] + fold(es),
@@ -369,7 +370,7 @@
         )
 
     zero = jnp.zeros((8, TOK), f32)
-    accs = lax.fori_loop(0, V // 56, stats, (zero, zero, zero, zero))
+    accs = lax.fori_loop(0, V // 24, stats, (zero, zero, zero, zero))
     for i in range(4):
         total_i = jnp.sum(accs[i], axis=0, keepdims=True)
         st[i : i + 1, :] = total_i[:, 0:256]
@@ -401,12 +402,10 @@
     scale[1:2, :] = 2.0 / zs
     for k in range(4):
         cols = slice(k * 128, (k + 1) * 128)
-        s = sb[:, cols]
         row_all = lax.broadcasted_iota(jnp.int32, (V, 128), 0)
         onehot = (row_all == token[:, cols]).astype(f32)
-        u = s / 30.0
         g = scale[1:2, cols] * esb[:, cols] - scale[0:1, cols] * etb[:, cols] - onehot
-        g = g * (1.0 - u * u) / TOK
+        g = g * sb[:, cols] * (1.0 / TOK)
         dz[:, cols] = g.astype(bf16)
         dzt[cols, :] = g.T.astype(bf16)
 
@@ -426,7 +425,7 @@
         ho[:, :, :, cols] = val
 
     every = slice(None)
-    chunks0 = [pl.ds(j * 512, 512) for j in range(HA // 512)]
+    chunks0 = [pl.ds(j, min(512, HA - j)) for j in range(0, HA, 512)]
     c_d0 = [Copy(hs.at[every, every, every, pl.ds(0, HB)], hr.at[every, every, every, pl.ds(0, HB)], sib)]
     c_d1 = [Copy(hs.at[every, every, every, ch], hr.at[every, every, every, ch], sib) for ch in chunks0]
     c_x1 = [
@@ -448,23 +447,34 @@
     def grad0():
         product(HA, HB, out_send)
         c_d0[0].start()
-        product(0, HA, out_own)
         for j, ch in enumerate(chunks0):
-            cols = slice(j * 512, (j + 1) * 512)
+            lo, n = ch.start, ch.size
+
+            def combine(i, _, lo=lo):
+                cols = pl.ds(pl.multiple_of(lo + i * 256, 256), 256)
+                val = dot(dzt[...], se[:, cols], 1, 0).reshape(NZ, NX, 16, 256)
+                ho[:, :, :, cols] = val
+                return 0
+
+            lax.fori_loop(0, n // 256, combine, 0)
             c_d1[j].wait_recv()
-            val = ho[:, :, :, cols] + hr[:, :, :, cols].astype(f32)
-            ho[:, :, :, cols] = val
-            hc[:, :, :, cols] = val.astype(bf16)
+            val = ho[:, :, :, ch] + hr[:, :, :, ch].astype(f32)
+            ho[:, :, :, ch] = val
+            hc[:, :, :, ch] = val.astype(bf16)
             for cp in c_x1[j]:
                 cp.start()
 
     def grad1():
-        for j, ch in enumerate(chunks0):
-            def one(cols, val, j=j):
-                hs[:, :, :, pl.ds(pl.multiple_of(cols.start + j * 512, 256), 256)] = val.astype(bf16)
-
-            product(j * 512, 512, one)
+        def part(j):
+            ch = chunks0[j]
+
+            def one(cols, val):
+                hs[:, :, :, pl.ds(pl.multiple_of(cols.start + ch.start, 256), 256)] = val.astype(bf16)
+
+            product(ch.start, ch.size, one)
             c_d1[j].start()
+
+        part(0)
         product(HA, HB, out_own)
         c_d0[0].wait_recv()
         val = ho[:, :, :, 0:HB] + hr[:, :, :, 0:HB].astype(f32)
@@ -472,6 +482,8 @@
         hc[:, :, :, 0:HB] = val.astype(bf16)
         c_za[0].start()
         c_zb[0].start()
+        for j in range(1, len(chunks0)):
+            part(j)
 
     on_core(0, grad0)
     on_core(1, grad1)
@@ -505,7 +517,7 @@
         def fn():
             for cp in c_x1[j]:
                 cp.wait_recv()
-            cols = slice(j * 512, (j + 1) * 512)
+            cols = chunks0[j]
             val = ho[:, x, :, cols]
             for k in range(3):
                 val = val + x1r[k, :, :, cols].astype(f32)
@@ -559,11 +571,11 @@
         for j in range(len(chunks0)):
             for cp in c_z2[j]:
                 cp.wait_recv()
-            cols = slice(j * 512, (j + 1) * 512)
+            cols = chunks0[j]
             val = y1[z, :, cols]
             for k in range(7):
                 val = val + z2r[k, :, cols].astype(f32)
-            for t in range(4):
+            for t in range(cols.size // 128):
                 fs0[:, 4 * j + t, :] = val[:, t * 128 : (t + 1) * 128]
         for cp in c_f0:
             cp.start()
@@ -608,7 +620,7 @@
 
     student_drain()
     teacher_drain()
-    for cp in [c_sh, c_f, c_s1, c_q1] + c_pr + c_s2 + c_s3 + c_q2 + c_q3:
+    for cp in [c_sh, c_r, c_a, c_q1] + c_pr + c_s2 + c_s3 + c_q2 + c_q3:
         cp.wait_send()
 
     def end0():
@@ -645,8 +657,8 @@
             v((NZ, NX, 16, DS), bf16), v((NZ, NX, 2 * F, TOK), bf16),
             v((8, DS), f32), v((8, DS), f32),
             v((NY, F, 128), f32), v((NY - 1, F, 128), f32), v((8, TOK), f32),
-            v((8, 128), f32), v((8, 128), f32), v((8, 128), f32), v((4, 8, 128), f32), v((7, 8, 128), f32),
-            v((F, 128), f32), v((F, 128), f32),
+            v((8, 128), f32), v((8, 128), f32), v((3, 8, 128), f32), v((7, 8, 128), f32),
+            v((F, 128), f32), v((F, 128), f32), v((F, 128), f32), v((F, 128), f32),
             v((V, TOK), f32), v((V, TOK), f32), v((V, TOK), f32), v((V, TOK), f32),
             v((8, 256), f32), v((8, 256), f32), v((8, 256), f32),
             v((8, 256), f32), v((15, 8, 256), f32), v((7, 8, 256), f32),

time: 114 us -> 118 us (1.035)
  Pallas kernels: 106 us -> 110 us
    pallas_call x1, Pallas kernels: 106 us -> 110 us  [body(): pl.pallas_call(kernel, out_shape=(jax.ShapeDtypeStruct((1, 1), f32), jax....]
where the time goes in v3:
time: 118 us
  Pallas kernels  110 us (93%)
  local copies, waits for them, and re-layouts  5.43 us (5%)
  between operations  2.33 us (2%)
    pallas_call x1, Pallas kernels, body(): pl.pallas_call(kernel, out_shape=(jax.ShapeDtypeStruct((1, 1), f32), jax....  110 us
    unnamed x2, local copies, waits for them, and re-layouts  5.43 us

profile of v3, /device:TPU:1, one launch (start us, length us, event | category | flops | bytes accessed | tf_op | source)
XLA Modules:
  0.0 117.6 jit_solution(15298321857997046898)
XLA Ops:
  0.6 109.9 %step.1 = (f32[1,1]{1,0:T(1,128)}, f32[2,3584]{1,0:T(2,128)}, bf16[504,3584]{1,0:T(8,128)(2,1)}) custom-call(bf16[512,512]{1,0:T(8,128)(2,1)} %attn_h.1, bf16[72,512]{1,0:T(8,128)(2,1)} %bitcast.4, bf16[72,512]{1,0:T(8,128)(2,1)} %bitcast.5, f32[2,4608]{1,0:T(2,128)} %gains_h.1, bf16[504,4608]{1,0:T(8,128)(2,1)} %te_h.1, bf16[8,3584]{1,0:T(8,128)(2,1)} %sh_h.1, ...), custom_call_target="tpu_custom_call" | custom-call | tf_op jit(solution)/shard_map/step/pallas_call | solution.py:645
  111.1 1.4 %copy.15 = f32[2,3584]{1,0:T(2,128)} copy(f32[2,3584]{1,0:T(2,128)} %get-tuple-element.13) | data formatting | bytes 57344
  112.4 4.1 %copy.16 = bf16[504,3584]{1,0:T(8,128)(2,1)} copy(bf16[504,3584]{1,0:T(8,128)(2,1)} %get-tuple-element.14) | data formatting | bytes 7225344

commit v4 on v3

--- a/solution.py
+++ b/solution.py
@@ -7,9 +7,9 @@
 
 TOK, DT, DS, V, F = 512, 4608, 3584, 504, 72
 NZ, NX, NY = 8, 4, 4
-SA = 1792
-TA = 64
-HA = 2304
+SA = 2048
+TA = 80
+HA = 2560
 HB = DS - HA
 NSEM = 320
 MESH = pl.DeviceIdType.MESH
@@ -26,7 +26,7 @@
     attn, oproj, resid, gains, te, sh, se, ids,
     sf, tf, shx, shr, pt, pr, scale, sums2, sums3, sr1, sr2, rx, rr, ax, ar,
     sb, tb, esb, etb, st, st2, st3, q1, q2, q3, dz, dzt,
-    ho, hs, hr, hc, x1r, za, zb, ta, tb2, y1, y1b, z2r, x2r, fs0, fs1, fr0, fr1, eg,
+    hs, hr, hc, x1r, z1r, y1, y1b, z2r, x2r, fs0, fs1, fr0, fr1, eg,
     lsem, ss, rs,
 ):
     w = lax.axis_index("wide")
@@ -95,14 +95,10 @@
         pl.semaphore_signal(barrier, inc=1, device_id=p, device_id_type=MESH)
     local[0].wait()
     shx[...] = sh[...].astype(f32)
-    pl.semaphore_wait(barrier, len(peers))
-
     c_sh = Copy(shx, shr, sib)
-    c_sh.start()
     local[3].wait()
     rx[...] = resid[:, pl.ds(pl.multiple_of(y * 128, 128), 128)].astype(f32)
     c_r = Copy(rx, rr, sib)
-    c_r.start()
 
     def ring(n, pos, peer, block, half):
         m = n // 2
@@ -221,8 +217,25 @@
     for b in range(NY):
         pt[b] = proj[:, b * 128 : (b + 1) * 128]
     c_pr = [Copy(pt.at[(y + k) % NY], pr.at[k - 1], yp(k)) for k in range(1, NY)]
+    local[4].wait()
+    feature = (w // 2) * 2 * F + lax.broadcasted_iota(jnp.int32, (2 * F, 128), 0)
+    lane = lax.broadcasted_iota(jnp.int32, (2 * F, 128), 1)
+
+    def pick_gains(i, carry):
+        part = gains[:, pl.ds(pl.multiple_of(i * 128, 128), 128)]
+        here = (lane + i * 128) == feature
+        return carry[0] + jnp.where(here, part[0:1, :], 0.0), carry[1] + jnp.where(here, part[1:2, :], 0.0)
+
+    none = jnp.zeros((2 * F, 128), f32)
+    g0, g1 = lax.fori_loop(0, DT // 128, pick_gains, (none, none))
+    g0 = jnp.sum(g0, axis=1, keepdims=True)
+    g1 = jnp.sum(g1, axis=1, keepdims=True)
+
+    pl.semaphore_wait(barrier, len(peers))
+    c_sh.start()
     for cp in c_pr:
         cp.start()
+    c_r.start()
 
     c_sh.wait_recv()
     first = jnp.where(c == 0, shx[...], shr[...])
@@ -237,21 +250,6 @@
 
     on_core(0, put0)
     on_core(1, put1)
-    next(student)
-
-    local[4].wait()
-    feature = (w // 2) * 2 * F + lax.broadcasted_iota(jnp.int32, (2 * F, 128), 0)
-    lane = lax.broadcasted_iota(jnp.int32, (2 * F, 128), 1)
-
-    def pick_gains(i, carry):
-        part = gains[:, pl.ds(pl.multiple_of(i * 128, 128), 128)]
-        here = (lane + i * 128) == feature
-        return carry[0] + jnp.where(here, part[0:1, :], 0.0), carry[1] + jnp.where(here, part[1:2, :], 0.0)
-
-    none = jnp.zeros((2 * F, 128), f32)
-    g0, g1 = lax.fori_loop(0, DT // 128, pick_gains, (none, none))
-    g0 = jnp.sum(g0, axis=1, keepdims=True)
-    g1 = jnp.sum(g1, axis=1, keepdims=True)
     next(student)
 
     def both_cores(own, other):
@@ -284,7 +282,6 @@
     for cp in c_s3:
         cp.start()
     next(student)
-    next(student)
     for cp in c_s3:
         cp.wait_recv()
     total = sums3[...] + jnp.sum(sr2[...], axis=0)
@@ -330,13 +327,16 @@
     next(student)
     next(teacher)
     next(student)
+    next(teacher)
+    next(student)
+    next(student)
 
     local[6].wait()
     for k in range(7):
         cols = slice(k * 512, (k + 1) * 512)
         part = dot(se[:, cols], sf[:, :, :, cols].reshape(TOK, 512), 1, 1)
         sb[...] = part if k == 0 else sb[...] + part
-        if k < 6:
+        if k in (0, 1, 2, 4, 6):
             next(teacher)
 
     local[7].wait()
@@ -382,12 +382,29 @@
     c_q2 = [Copy(st2, q2.at[k - 1], xyp(k)) for k in range(1, 16)]
     for cp in c_q2:
         cp.start()
+    student_drain()
+    for cp in [c_sh, c_r, c_a, c_q1] + c_pr + c_s2 + c_s3:
+        cp.wait_send()
     for cp in c_q2:
         cp.wait_recv()
     st3[...] = st2[...] + jnp.sum(q2[...], axis=0)
     c_q3 = [Copy(st3, q3.at[k - 1], zp(k)) for k in range(1, 8)]
     for cp in c_q3:
         cp.start()
+    teacher_drain()
+
+    def spread_sent0():
+        for cp in c_y0:
+            cp.wait_send()
+
+    def spread_sent1():
+        for cp in c_y1:
+            cp.wait_send()
+
+    on_core(0, spread_sent0)
+    on_core(1, spread_sent1)
+    for cp in c_q2:
+        cp.wait_send()
     for cp in c_q3:
         cp.wait_recv()
     packed = st3[...] + jnp.sum(q3[...], axis=0)
@@ -421,9 +438,6 @@
     def out_send(cols, val):
         hs[:, :, :, cols] = val.astype(bf16)
 
-    def out_own(cols, val):
-        ho[:, :, :, cols] = val
-
     every = slice(None)
     chunks0 = [pl.ds(j, min(512, HA - j)) for j in range(0, HA, 512)]
     c_d0 = [Copy(hs.at[every, every, every, pl.ds(0, HB)], hr.at[every, every, every, pl.ds(0, HB)], sib)]
@@ -433,34 +447,24 @@
         for ch in chunks0
     ]
     own_b = pl.ds(0, HB)
-    half_b = (pl.ds(0, HB // 2), pl.ds(HB // 2, HB // 2))
-
-    def zi(k):
-        return (z + k + NZ) % NZ
-
-    c_za = [Copy(hc.at[zi(4), every, every, half_b[0]], za.at[0, every, every, half_b[0]], zp(1))]
-    c_zb = [Copy(hc.at[zi(4), every, every, half_b[1]], zb.at[0, every, every, half_b[1]], zp(-1))]
-    for k in range(1, 4):
-        c_za.append(Copy(ta.at[k - 1], za.at[k], zp(1)))
-        c_zb.append(Copy(tb2.at[k - 1], zb.at[k], zp(-1)))
+    c_z1 = [Copy(hc.at[(z + k) % NZ, every, every, own_b], z1r.at[k - 1], zp(k)) for k in (4, 1, 7, 2, 6, 3, 5)]
+
+    def combined(lo, n, at):
+        def step(i, _):
+            cols = pl.ds(pl.multiple_of(lo + i * 256, 256), 256)
+            here = pl.ds(pl.multiple_of(at + i * 256, 256), 256)
+            val = dot(dzt[...], se[:, cols], 1, 0).reshape(NZ, NX, 16, 256)
+            hc[:, :, :, here] = (val + hr[:, :, :, here].astype(f32)).astype(bf16)
+            return 0
+
+        lax.fori_loop(0, n // 256, step, 0)
 
     def grad0():
         product(HA, HB, out_send)
         c_d0[0].start()
         for j, ch in enumerate(chunks0):
-            lo, n = ch.start, ch.size
-
-            def combine(i, _, lo=lo):
-                cols = pl.ds(pl.multiple_of(lo + i * 256, 256), 256)
-                val = dot(dzt[...], se[:, cols], 1, 0).reshape(NZ, NX, 16, 256)
-                ho[:, :, :, cols] = val
-                return 0
-
-            lax.fori_loop(0, n // 256, combine, 0)
             c_d1[j].wait_recv()
-            val = ho[:, :, :, ch] + hr[:, :, :, ch].astype(f32)
-            ho[:, :, :, ch] = val
-            hc[:, :, :, ch] = val.astype(bf16)
+            combined(ch.start, ch.size, ch.start)
             for cp in c_x1[j]:
                 cp.start()
 
@@ -475,14 +479,12 @@
             c_d1[j].start()
 
         part(0)
-        product(HA, HB, out_own)
+        part(1)
         c_d0[0].wait_recv()
-        val = ho[:, :, :, 0:HB] + hr[:, :, :, 0:HB].astype(f32)
-        ho[:, :, :, 0:HB] = val
-        hc[:, :, :, 0:HB] = val.astype(bf16)
-        c_za[0].start()
-        c_zb[0].start()
-        for j in range(1, len(chunks0)):
+        combined(HA, HB, 0)
+        for cp in c_z1:
+            cp.start()
+        for j in range(2, len(chunks0)):
             part(j)
 
     on_core(0, grad0)
@@ -518,7 +520,7 @@
             for cp in c_x1[j]:
                 cp.wait_recv()
             cols = chunks0[j]
-            val = ho[:, x, :, cols]
+            val = hc[:, x, :, cols].astype(f32)
             for k in range(3):
                 val = val + x1r[k, :, :, cols].astype(f32)
             y1[:, :, cols] = val
@@ -528,28 +530,12 @@
 
         return fn
 
-    def first1(n):
-        def fn():
-            c_za[n - 1].wait_recv()
-            c_zb[n - 1].wait_recv()
-            a_, b_ = half_b
-            if n == 1:
-                ta[0, :, :, a_] = (ho[zi(3), :, :, a_] + za[0, :, :, a_].astype(f32)).astype(bf16)
-                ta[0, :, :, b_] = hc[zi(3), :, :, b_]
-                tb2[0, :, :, a_] = hc[zi(-3), :, :, a_]
-                tb2[0, :, :, b_] = (ho[zi(-3), :, :, b_] + zb[0, :, :, b_].astype(f32)).astype(bf16)
-            else:
-                ta[n - 1] = (ho[zi(4 - n), :, :, own_b] + za[n - 1].astype(f32)).astype(bf16)
-                tb2[n - 1] = (ho[zi(n - 4), :, :, own_b] + zb[n - 1].astype(f32)).astype(bf16)
-            c_za[n].start()
-            c_zb[n].start()
-
-        return fn
-
     def turn1():
-        c_za[3].wait_recv()
-        c_zb[3].wait_recv()
-        val = ho[z, :, :, own_b] + za[3].astype(f32) + zb[3].astype(f32)
+        for cp in c_z1:
+            cp.wait_recv()
+        val = hc[z, :, :, own_b].astype(f32)
+        for k in range(7):
+            val = val + z1r[k].astype(f32)
         y1[0:NX, :, own_b] = val
         y1b[0:NX, :, own_b] = val.astype(bf16)
         for cp in c_x2b:
@@ -584,12 +570,30 @@
     for k in range(2):
         embed(k)
     for n, (f0, f1) in enumerate(
-        [(first0(0), first1(1)), (first0(1), first1(2)), (first0(2), first1(3)), (first0(3), turn1), (first0(4), last1)]
+        [(first0(0), None), (first0(1), None), (first0(2), None), (first0(3), turn1), (first0(4), None)]
     ):
         on_core(0, f0)
-        on_core(1, f1)
+        if f1 is not None:
+            on_core(1, f1)
         embed(2 + n)
     on_core(0, last0)
+    on_core(1, last1)
+
+    for cp in c_q3:
+        cp.wait_send()
+
+    def end0():
+        for cp in c_d0 + [b for a_ in c_x1 + c_z2 for b in a_]:
+            cp.wait_send()
+
+    def end1():
+        for cp in c_d1 + c_z1 + c_x2b:
+            cp.wait_send()
+
+    on_core(0, end0)
+    on_core(1, end1)
+    for cp in c_eg:
+        cp.wait()
 
     def arrive(frx, k, i):
         pltpu.make_async_remote_copy(
@@ -618,23 +622,16 @@
         piece = head[:, t, :] if t < HA // 128 else tail[:, t - HA // 128, :]
         hg_o[:, t * 128 : (t + 1) * 128] = piece
 
-    student_drain()
-    teacher_drain()
-    for cp in [c_sh, c_r, c_a, c_q1] + c_pr + c_s2 + c_s3 + c_q2 + c_q3:
-        cp.wait_send()
-
-    def end0():
-        for cp in c_y0 + c_d0 + [b for a_ in c_x1 + c_z2 for b in a_] + c_f0:
+    def sent0():
+        for cp in c_f0:
             cp.wait_send()
 
-    def end1():
-        for cp in c_y1 + c_d1 + c_za + c_zb + c_x2b + c_f1:
+    def sent1():
+        for cp in c_f1:
             cp.wait_send()
 
-    on_core(0, end0)
-    on_core(1, end1)
-    for cp in c_eg:
-        cp.wait()
+    on_core(0, sent0)
+    on_core(1, sent1)
     assert counter[0] <= NSEM
 
 
@@ -663,9 +660,9 @@
             v((8, 256), f32), v((8, 256), f32), v((8, 256), f32),
             v((8, 256), f32), v((15, 8, 256), f32), v((7, 8, 256), f32),
             v((V, TOK), bf16), v((TOK, V), bf16),
-            v((NZ, NX, 16, HA), f32), v((NZ, NX, 16, HA), bf16), v((NZ, NX, 16, HA), bf16), v((NZ, NX, 16, HA), bf16),
+            v((NZ, NX, 16, HA), bf16), v((NZ, NX, 16, HA), bf16), v((NZ, NX, 16, HA), bf16),
             v((3, NZ, 16, HA), bf16),
-            v((4, NX, 16, HB), bf16), v((4, NX, 16, HB), bf16), v((3, NX, 16, HB), bf16), v((3, NX, 16, HB), bf16),
+            v((7, NX, 16, HB), bf16),
             v((NZ, 16, HA), f32), v((NZ, 16, HA), bf16), v((7, 16, HA), bf16), v((4, 16, HB), bf16),
             v((16, HA // 128, 128), f32), v((16, HB // 128, 128), f32),
             v((4, 2, HA // 128, 128), f32), v((4, 2, HB // 128, 128), f32),

time: 118 us -> 112 us (0.949)
  Pallas kernels: 110 us -> 104 us
    pallas_call x1, Pallas kernels: 110 us -> 104 us  [body(): pl.pallas_call(kernel, out_shape=(jax.ShapeDtypeStruct((1, 1), f32), jax....]
where the time goes in v4:
time: 112 us
  Pallas kernels  104 us (93%)
  local copies, waits for them, and re-layouts  5.43 us (5%)
  between operations  2.33 us (2%)
    pallas_call x1, Pallas kernels, body(): pl.pallas_call(kernel, out_shape=(jax.ShapeDtypeStruct((1, 1), f32), jax....  104 us
    unnamed x2, local copies, waits for them, and re-layouts  5.43 us

profile of v4, /device:TPU:1, one launch (start us, length us, event | category | flops | bytes accessed | tf_op | source)
XLA Modules:
  0.0 111.7 jit_solution(921215013480966044)
XLA Ops:
  0.6 104.0 %step.1 = (f32[1,1]{1,0:T(1,128)}, f32[2,3584]{1,0:T(2,128)}, bf16[504,3584]{1,0:T(8,128)(2,1)}) custom-call(bf16[512,512]{1,0:T(8,128)(2,1)} %attn_h.1, bf16[72,512]{1,0:T(8,128)(2,1)} %bitcast.4, bf16[72,512]{1,0:T(8,128)(2,1)} %bitcast.5, f32[2,4608]{1,0:T(2,128)} %gains_h.1, bf16[504,4608]{1,0:T(8,128)(2,1)} %te_h.1, bf16[8,3584]{1,0:T(8,128)(2,1)} %sh_h.1, ...), custom_call_target="tpu_custom_call" | custom-call | tf_op jit(solution)/shard_map/step/pallas_call | solution.py:642
  105.2 1.4 %copy.15 = f32[2,3584]{1,0:T(2,128)} copy(f32[2,3584]{1,0:T(2,128)} %get-tuple-element.13) | data formatting | bytes 57344
  106.5 4.1 %copy.16 = bf16[504,3584]{1,0:T(8,128)(2,1)} copy(bf16[504,3584]{1,0:T(8,128)(2,1)} %get-tuple-element.14) | data formatting | bytes 7225344

commit v5 on v4

--- a/solution.py
+++ b/solution.py
@@ -8,8 +8,8 @@
 TOK, DT, DS, V, F = 512, 4608, 3584, 504, 72
 NZ, NX, NY = 8, 4, 4
 SA = 2048
-TA = 80
-HA = 2560
+TA = 64
+HA = 2816
 HB = DS - HA
 NSEM = 320
 MESH = pl.DeviceIdType.MESH
@@ -570,14 +570,17 @@
     for k in range(2):
         embed(k)
     for n, (f0, f1) in enumerate(
-        [(first0(0), None), (first0(1), None), (first0(2), None), (first0(3), turn1), (first0(4), None)]
+        [
+            (first0(0), None), (first0(1), None), (first0(2), turn1),
+            (first0(3), None), (first0(4), last1), (first0(5), None),
+        ]
     ):
         on_core(0, f0)
         if f1 is not None:
             on_core(1, f1)
-        embed(2 + n)
+        if n < 5:
+            embed(2 + n)
     on_core(0, last0)
-    on_core(1, last1)
 
     for cp in c_q3:
         cp.wait_send()

time: 112 us -> 112 us (level)
  no operation moved by 1% of the time
where the time goes in v5:
time: 112 us; the launch traced here: 111 us
  Pallas kernels  104 us (93%)
  local copies, waits for them, and re-layouts  5.43 us (5%)
  between operations  2.33 us (2%)
    pallas_call x1, Pallas kernels, body(): pl.pallas_call(kernel, out_shape=(jax.ShapeDtypeStruct((1, 1), f32), jax....  104 us
    unnamed x2, local copies, waits for them, and re-layouts  5.43 us

profile of v5, /device:TPU:1, one launch (start us, length us, event | category | flops | bytes accessed | tf_op | source)
XLA Modules:
  0.0 111.4 jit_solution(7377527634217355749)
XLA Ops:
  0.6 103.7 %step.1 = (f32[1,1]{1,0:T(1,128)}, f32[2,3584]{1,0:T(2,128)}, bf16[504,3584]{1,0:T(8,128)(2,1)}) custom-call(bf16[512,512]{1,0:T(8,128)(2,1)} %attn_h.1, bf16[72,512]{1,0:T(8,128)(2,1)} %bitcast.4, bf16[72,512]{1,0:T(8,128)(2,1)} %bitcast.5, f32[2,4608]{1,0:T(2,128)} %gains_h.1, bf16[504,4608]{1,0:T(8,128)(2,1)} %te_h.1, bf16[8,3584]{1,0:T(8,128)(2,1)} %sh_h.1, ...), custom_call_target="tpu_custom_call" | custom-call | tf_op jit(solution)/shard_map/step/pallas_call | solution.py:645
  104.8 1.4 %copy.15 = f32[2,3584]{1,0:T(2,128)} copy(f32[2,3584]{1,0:T(2,128)} %get-tuple-element.13) | data formatting | bytes 57344
  106.2 4.1 %copy.16 = bf16[504,3584]{1,0:T(8,128)(2,1)} copy(bf16[504,3584]{1,0:T(8,128)(2,1)} %get-tuple-element.14) | data formatting | bytes 7225344
